TPU v7x, 256 devices: a whole 4x4x8 slice. The times are simulated.
256 devices in a mesh: expert: 8 (over x_hi, y), tensor: 32 (over z, x_lo, core).
Axes of the slice: x: 4 (x_hi: 2, x_lo: 2; x = x_hi * 2 + x_lo), y: 4, z: 8, core: 2. Of those that a mesh axis runs over, the one named last changes fastest.
Arguments:
- tokens: bfloat16 [4096, 3072], P('tensor'), may hold values from -6 to 6
- routes: int32 [4096, 2], P('tensor'), may hold values from 0 to 7, all different within a row; in each aligned block of 128 rows (0 to 127, 128 to 255, ...) at most 40 rows name the same one
- gates: float32 [4096, 2], P('tensor'), may hold values from 0.2 to 1
- gate_w: bfloat16 [8, 16384, 3072], P(None, ('expert', 'tensor')), may hold values from -0.109375 to 0.109375
- up_w: bfloat16 [8, 16384, 3072], P(None, ('expert', 'tensor')), may hold values from -0.109375 to 0.109375
- down_w: bfloat16 [8, 16384, 3072], P(None, ('expert', 'tensor')), may hold values from -0.046875 to 0.046875
Outputs:
- mixed: bfloat16 [4096, 3072], P('tensor')
Inputs may be any that keep to these rules, and one draw needn't show every extreme that they name: `routes`: in each aligned block of 128 rows (the rows of one tensor index) the 2 experts of a row differ, no expert is named by more than 40 rows, a bound that some block reaches.
All inputs are finite; a program needn't handle non-finite values.
Results may differ from a plain program's by a relative error of at most 0.0058.
Values may be sent and summed in bfloat16 or wider, within the bound.
No kernel may reach another device: no remote copies, remote signals or barrier semaphores. Data moves between devices by JAX's collectives and lax.ppermute only.
A program may use at most 128 MiB of HBM per device.

v0:
```python
import jax
import jax.numpy as jnp
from jax import lax
from jax.sharding import PartitionSpec as P


def slot_tables(routes, gates, expert_count, capacity):
    labels = jnp.arange(expert_count, dtype=jnp.int32)
    matches_all = routes[None, :, :] == labels[:, None, None]
    member = jnp.any(matches_all, axis=2)
    weight = jnp.sum(
        jnp.where(matches_all, gates[None, :, :], jnp.zeros_like(gates)[None, :, :]), axis=2
    )
    position = jnp.cumsum(member.astype(jnp.int32), axis=1) - 1
    places = jnp.arange(capacity, dtype=jnp.int32)
    onehot = jnp.logical_and(position[:, None, :] == places[None, :, None], member[:, None, :])
    return (onehot.astype(jnp.float32), weight)


def swiglu(selected, gate_matrix, up_matrix):
    contract = (((1,), (1,)), ((), ()))
    gated = lax.dot_general(selected, gate_matrix, contract, preferred_element_type=jnp.float32)
    upward = lax.dot_general(selected, up_matrix, contract, preferred_element_type=jnp.float32)
    return (jax.nn.silu(gated) * upward).astype(jnp.bfloat16)


def per_device(tokens, routes, gates, gate_w, up_w, down_w):
    expert_count = lax.axis_size("expert")
    tok_rows = tokens.shape[0]
    capacity = 5 * tok_rows * routes.shape[1] // (4 * expert_count)
    gate_own, up_own, down_own = (
        lax.all_to_all(gate_w, "expert", split_axis=0, concat_axis=1, tiled=True),
        lax.all_to_all(up_w, "expert", split_axis=0, concat_axis=1, tiled=True),
        lax.all_to_all(down_w, "expert", split_axis=0, concat_axis=1, tiled=True),
    )
    down_own = down_own[0]
    gate_own = gate_own[0]
    up_own = up_own[0]
    onehot, weight = slot_tables(routes, gates, expert_count, capacity)
    expert = lax.axis_index("expert")
    chosen = lax.dynamic_index_in_dim(onehot, expert, 0, keepdims=False)
    picked = jnp.dot(
        chosen.astype(jnp.bfloat16), tokens, preferred_element_type=jnp.float32
    ).astype(jnp.bfloat16)
    hidden = swiglu(lax.all_gather(picked, "tensor", axis=0, tiled=True), gate_own, up_own)
    summed = lax.psum_scatter(
        jnp.dot(hidden, down_own, preferred_element_type=jnp.float32),
        "tensor",
        scatter_dimension=0,
        tiled=True,
    )
    expert_out = summed.astype(jnp.bfloat16)
    own_weight = lax.dynamic_index_in_dim(weight, expert, 0, keepdims=False)
    scaled = chosen * own_weight[None, :]
    placed = jnp.einsum(
        "ct,cd->td", scaled, expert_out.astype(jnp.float32), precision=lax.Precision.HIGHEST
    )
    mixed = lax.psum(placed, "expert")
    return mixed.astype(jnp.bfloat16)


def solution(mesh):
    placed = (
        P("tensor", None),
        P("tensor", None),
        P("tensor", None),
        P(None, ("expert", "tensor"), None),
        P(None, ("expert", "tensor"), None),
        P(None, ("expert", "tensor"), None),
    )
    return jax.shard_map(
        per_device, mesh=mesh, in_specs=placed, out_specs=P("tensor", None), check_vma=False
    )
```

profile of v0, /device:TPU:24, one launch (start us, length us, event | category | flops | bytes accessed | tf_op | source)
XLA Modules:
  0.0 451.4 jit_solution(11547333939608472171)
XLA Ops:
  6.5 0.0 copy-start
  6.5 0.0 all-gather.2.cloned.1.call-start
  6.5 0.8 fusion.11
  7.3 0.3 reduce_window_sum.11
  7.6 0.1 copy-done
  7.7 0.9 convolution_convert_fusion
  8.6 0.0 all-gather.2.cloned.1.call-update
  8.6 0.0 copy-start.1
  8.7 71.9 %all_to_all.12 = bf16[8,64,3072]{2,1,0:T(8,128)(2,1)} all-to-all(bf16[8,64,3072]{2,1,0:T(8,128)(2,1)} %param.9), channel_id=1, replica_groups=mesh['expert'=8,'tensor'=32] {'expert'}, dimensions={0} | all-to-all | bytes 6291456 | tf_op jit(solution)/shard_map/all_to_all | solution.py:32
  80.6 0.0 copy-done.1
  80.6 46.2 %all_to_all.13 = bf16[8,64,3072]{2,1,0:T(8,128)(2,1)} all-to-all(bf16[8,64,3072]{2,1,0:T(8,128)(2,1)S(1)} %copy-done.1), channel_id=1, replica_groups=mesh['expert'=8,'tensor'=32] {'expert'}, dimensions={0} | all-to-all | bytes 6291456 | tf_op jit(solution)/shard_map/all_to_all | solution.py:33
  126.8 6.8 %all-to-all-start.2 = ((bf16[8,64,3072]{2,1,0:T(8,128)(2,1)}), bf16[8,64,3072]{2,1,0:T(8,128)(2,1)}, u32[]{:S(2)}, u32[]{:S(2)}) async-start(bf16[8,64,3072]{2,1,0:T(8,128)(2,1)} %param.11), calls=%async_computation.2 | async-start | bytes 6291456 | tf_op jit(solution)/shard_map/all_to_all | solution.py:34
  133.6 0.0 reduce-scatter.2.cloned.1.call-start
  133.6 0.0 all-gather.2.cloned.1.call-done
  133.6 9.9 %fusion.14 = f32[1280,512]{1,0:T(8,128)} fusion(bf16[1280,3072]{1,0:T(8,128)(2,1)} %all-gather.2.cloned.1.call-done, bf16[512,3072]{1,0:T(8,128)(2,1)} %bitcast.17), kind=kOutput, calls=%fused_computation.24 | convolution fusion | flops 4026531840 | bytes 13631488 | tf_op jit(solution)/shard_map/dot_general | solution.py:22
  143.4 24.9 %all-to-all-done.2 = bf16[8,64,3072]{2,1,0:T(8,128)(2,1)} async-done(((bf16[8,64,3072]{2,1,0:T(8,128)(2,1)}), bf16[8,64,3072]{2,1,0:T(8,128)(2,1)}, u32[]{:S(2)}, u32[]{:S(2)}) %all-to-all-start.2) | async-done | bytes 3145760 | tf_op jit(solution)/shard_map/all_to_all | solution.py:34
  168.4 16.3 %fusion.1 = f32[1280,3072]{1,0:T(8,128)} fusion(bf16[512,3072]{1,0:T(8,128)(2,1)} %bitcast.4, bf16[1280,3072]{1,0:T(8,128)(2,1)} %all-gather.2.cloned.1.call-done, bf16[512,3072]{1,0:T(8,128)(2,1)} %bitcast.16, f32[1280,512]{1,0:T(8,128)} %fusion.14), kind=kOutput, calls=%fused_computation.3 | convolution fusion | flops 8056995840 | bytes 32505856 | tf_op jit(solution)/shard_map/dot_general | solution.py:47
  184.7 0.0 copy-start.2
  184.7 0.0 copy-start.3
  184.7 0.0 reduce-scatter.2.cloned.1.call-update
  184.7 0.7 copy-done.2
  185.3 0.0 copy-done.3
  185.4 177.3 %reduce-scatter.2.cloned.1.call-done = f32[40,3072]{1,0:T(8,128)} async-done(((f32[1280,3072]{1,0:T(8,128)}), f32[40,3072]{1,0:T(8,128)}) %reduce-scatter.2.cloned.1.call-update) | async-done | bytes 491536 | tf_op jit(solution)/shard_map/reduce_scatter | solution.py:46
  362.6 1.9 fusion.2
  364.5 80.0 %all-reduce.1 = bf16[128,3072]{1,0:T(8,128)(2,1)} all-reduce(f32[128,3072]{1,0:T(8,128)S(1)} %fusion.2), channel_id=1, replica_groups=mesh['expert'=8,'tensor'=32] {'expert'}, use_global_device_ids=true, to_apply=%region_4.5 | all-reduce | flops 393216 | bytes 2359296 | tf_op jit(solution)/shard_map/psum | solution.py:58
  (6 shorter events, 0.0 us)
Async XLA Ops:
  6.5 1.1 copy-start
  6.5 127.0 %all-gather.2.cloned.1.call-start = ((), (), s32[]{:S(2)}) async-start(), calls=%async_computation.4 | async-start | bytes 8110080 | tf_op jit(solution)/shard_map/all_gather | solution.py:45
  8.6 71.9 %copy-start.1 = (bf16[8,64,3072]{2,1,0:T(8,128)(2,1)S(1)}, bf16[8,64,3072]{2,1,0:T(8,128)(2,1)}, u32[]{:S(2)}) copy-start(bf16[8,64,3072]{2,1,0:T(8,128)(2,1)} %param.10) | copy-start | bytes 9437188
  126.8 41.6 %all-to-all-start.2 = ((bf16[8,64,3072]{2,1,0:T(8,128)(2,1)}), bf16[8,64,3072]{2,1,0:T(8,128)(2,1)}, u32[]{:S(2)}, u32[]{:S(2)}) async-start(bf16[8,64,3072]{2,1,0:T(8,128)(2,1)} %param.11), calls=%async_computation.2 | async-start | bytes 6291456 | tf_op jit(solution)/shard_map/all_to_all | solution.py:34
  133.6 229.1 %reduce-scatter.2.cloned.1.call-start = ((), (), s32[]{:S(2)}) async-start(), calls=%async_computation.5 | async-start | bytes 16220160 | tf_op jit(solution)/shard_map/reduce_scatter | solution.py:46
  184.7 0.7 copy-start.2
  184.7 0.7 copy-start.3
Sparse Core Ops, SparseCore 0:
  9.2 91.6 all-gather.1
  184.8 177.7 reduce-scatter.1
where the time goes:
time: 453 us; the launch traced here: 451 us
  waiting for transfers between devices  202 us (45%)
  blocking collectives  198 us (44%)
  matrix products  29 us (6%)
  between operations  13.4 us (3%)
  starting transfers between devices  6.77 us (1%)
    reduce_scatter x1, waiting for transfers between devices, per_device(): lax.psum_scatter(jnp.dot(hidden, down_own, preferred_element_type=jnp.flo...  177 us
    psum x1, blocking collectives, per_device(): mixed = lax.psum(placed, 'expert')  80 us
    all_to_all x1, blocking collectives, per_device(): lax.all_to_all(gate_w, 'expert', split_axis=0, concat_axis=1, tiled=True)  71.9 us
    all_to_all x1, blocking collectives, per_device(): lax.all_to_all(up_w, 'expert', split_axis=0, concat_axis=1, tiled=True)  46.2 us
    all_to_all x1, waiting for transfers between devices, per_device(): lax.all_to_all(down_w, 'expert', split_axis=0, concat_axis=1, tiled=True)  24.9 us
    dot_general x1, matrix products, per_device(): jnp.dot(hidden, down_own, preferred_element_type=jnp.float32)  16.3 us
    dot_general x1, matrix products, swiglu(): lax.dot_general(selected, gate_matrix, contract, preferred_element_type=j...  9.87 us
  transfers between devices with their start and end apart: 3, of which 2 were waited for; matrix products, arithmetic and copies ran while one was open for 2% of the time, Pallas kernels for 0%

commit v1 on v0

v1 whole, which is shorter than its diff:
```python
import jax
import jax.numpy as jnp
from jax import lax
from jax.experimental import pallas as pl
from jax.experimental.pallas import tpu as pltpu
from jax.sharding import PartitionSpec as P

CHUNKS = (1536, 1536)
EARLY = 32
ROW_TILE = 640


def slot_tables(routes, gates, expert_count, capacity):
    labels = jnp.arange(expert_count, dtype=jnp.int32)
    matches_all = routes[None, :, :] == labels[:, None, None]
    member = jnp.any(matches_all, axis=2)
    weight = jnp.sum(
        jnp.where(matches_all, gates[None, :, :], jnp.zeros_like(gates)[None, :, :]), axis=2
    )
    position = jnp.cumsum(member.astype(jnp.int32), axis=1) - 1
    places = jnp.arange(capacity, dtype=jnp.int32)
    onehot = jnp.logical_and(position[:, None, :] == places[None, :, None], member[:, None, :])
    return (onehot.astype(jnp.float32), weight)


def along_z(step, flip=0):
    return [(t, ((t ^ flip) + 4 * step) % 32) for t in range(32)]


X_LO = [(t, t ^ 2) for t in range(32)]
CORE = [(t, t ^ 1) for t in range(32)]


X_HI = [(e, e ^ 4) for e in range(8)]


def from_y(step):
    return [(e // 4 * 4 + (e % 4 + step) % 4, e) for e in range(8)]


def add(a, b):
    return a.astype(jnp.float32) + b.astype(jnp.float32)


def swiglu_kernel(rows_ref, gate_ref, up_ref, out_ref):
    contract = (((1,), (1,)), ((), ()))
    rows = rows_ref[...]
    gate = gate_ref[...].reshape(-1, rows.shape[1])
    up = up_ref[...].reshape(-1, rows.shape[1])
    gated = lax.dot_general(rows, gate, contract, preferred_element_type=jnp.float32)
    upward = lax.dot_general(rows, up, contract, preferred_element_type=jnp.float32)
    out_ref[...] = (gated / (1.0 + jnp.exp(-gated)) * upward).astype(out_ref.dtype)


def swiglu(rows, weights, depth):
    count, width = rows.shape
    sources = weights.shape[0] // 2
    step = sources * depth
    return pl.pallas_call(
        swiglu_kernel,
        grid=(2, count // ROW_TILE),
        in_specs=[
            pl.BlockSpec((ROW_TILE, width), lambda i, j: (j, 0)),
            pl.BlockSpec((sources, depth, width), lambda i, j: (i, 0, 0)),
            pl.BlockSpec((sources, depth, width), lambda i, j: (i, 1, 0)),
        ],
        out_specs=pl.BlockSpec((ROW_TILE, step), lambda i, j: (j, i)),
        out_shape=jax.ShapeDtypeStruct((count, 2 * step), rows.dtype),
        compiler_params=pltpu.CompilerParams(vmem_limit_bytes=60 * 2**20),
        cost_estimate=pl.CostEstimate(flops=1000, bytes_accessed=1000, transcendentals=0),
    )(rows, weights, weights)


def per_device(tokens, routes, gates, gate_w, up_w, down_w):
    expert_count = lax.axis_size("expert")
    tok_rows, width = tokens.shape
    capacity = 5 * tok_rows * routes.shape[1] // (4 * expert_count)
    expert = lax.axis_index("expert")
    bf16 = jnp.bfloat16

    def tensor_move(value, pairs):
        return lax.ppermute(value, "tensor", pairs)

    def expert_move(value, pairs):
        return lax.ppermute(value, "expert", pairs)

    def to_groups(matrix):
        return lax.all_to_all(matrix, "expert", split_axis=0, concat_axis=1, tiled=True)[0]

    with jax.named_scope("pick"):
        onehot, weight = slot_tables(routes, gates, expert_count, capacity)
        chosen = lax.dynamic_index_in_dim(onehot, expert, 0, keepdims=False)
        picked = jnp.dot(
            chosen.astype(bf16), tokens, preferred_element_type=jnp.float32
        ).astype(bf16)
        own = jnp.concatenate([picked, tensor_move(picked, X_LO)], axis=0)
        early = jnp.concatenate([gate_w, up_w, down_w[:, :EARLY]], axis=1)
        own, early, down_w = lax.optimization_barrier((own, early, down_w))

    unit = own.shape[0]
    half = width // 2
    with jax.named_scope("gate_up"):
        early = to_groups(early)
        late = down_w[:, EARLY:]
        block = {0: own}
        for k in (1, -1, 2, -2):
            block[k] = tensor_move(own, along_z(-k))
        block[3] = tensor_move(block[2], along_z(-1))
        block[-3] = tensor_move(block[-2], along_z(1))
        block[4] = jnp.concatenate(
            [
                tensor_move(block[2][:, :half], along_z(-2)),
                tensor_move(block[-2][:, half:], along_z(2)),
            ],
            axis=1,
        )
        order = (0, 1, -1, 2, -2, 3, -3, 4)
        near = jnp.concatenate([block[k] for k in order[:5]], axis=0)
        far = jnp.concatenate([block[k] for k in order[5:]], axis=0)
        rows = jnp.concatenate(
            [near, far, tensor_move(near, CORE), tensor_move(far, CORE)], axis=0
        )
        early, rows, late = lax.optimization_barrier((early, rows, late))

    with jax.named_scope("hidden"):
        late = to_groups(late)
        depth = gate_w.shape[1]
        early = early.reshape(expert_count, -1, width)
        hidden = swiglu(rows, early, depth)

        late, hidden = lax.optimization_barrier((late, hidden))
        late = late.reshape(expert_count, -1, width)
        down_own = jnp.concatenate([early[:, 2 * depth :], late], axis=1).reshape(-1, width)

    own_rows = rows.shape[0] // 2
    edges = [sum(CHUNKS[:n]) for n in range(len(CHUNKS) + 1)]
    columns = [down_own[:, a:b] for a, b in zip(edges[:-1], edges[1:])]
    with jax.named_scope("down"):
        theirs = [
            jnp.dot(hidden[own_rows:], c, preferred_element_type=jnp.float32).astype(bf16)
            for c in columns
        ]
        received = [tensor_move(t, CORE) for t in theirs]
        hidden_mine, _ = lax.optimization_barrier((hidden[:own_rows], theirs))
        totals = []
        for c, got in zip(columns, received):
            mine = jnp.dot(hidden_mine, c, preferred_element_type=jnp.float32)
            totals.append((mine + got.astype(jnp.float32)).astype(bf16))

    def chains(total, longer):
        size = total.shape[0] // 8
        part = {k: total[i * size : (i + 1) * size] for i, k in enumerate(order)}
        moving = {longer: tensor_move(part[4], along_z(longer))}
        for k in (3, 2):
            for way in (longer, -longer):
                here = part[way * k]
                if way in moving:
                    here = add(moving[way], here).astype(bf16)
                moving[way] = tensor_move(here, along_z(way))
        summed = part[0][:capacity].astype(jnp.float32)
        summed = add(summed, tensor_move(part[0][capacity:], X_LO))
        for way in (longer, -longer):
            here = add(moving[way], part[way]).astype(bf16)
            summed = add(summed, tensor_move(here[:capacity], along_z(way)))
            summed = add(summed, tensor_move(here[capacity:], along_z(way, 2)))
        return summed.astype(bf16)

    with jax.named_scope("scatter"):
        outs = [chains(t, 1 if n % 2 == 0 else -1) for n, t in enumerate(totals)]

    with jax.named_scope("mix"):
        scaled = onehot * weight[:, None, :]
        expert_out = jnp.concatenate(outs, axis=1)
        copies = jnp.broadcast_to(expert_out[None], (expert_count,) + expert_out.shape)
        return lax.dot_general(
            scaled.reshape(-1, tok_rows),
            to_groups(copies).astype(jnp.float32),
            (((0,), (0,)), ((), ())),
            precision=lax.Precision.HIGHEST,
            preferred_element_type=jnp.float32,
        ).astype(bf16)


def solution(mesh):
    placed = (
        P("tensor", None),
        P("tensor", None),
        P("tensor", None),
        P(None, ("expert", "tensor"), None),
        P(None, ("expert", "tensor"), None),
        P(None, ("expert", "tensor"), None),
    )
    return jax.shard_map(
        per_device, mesh=mesh, in_specs=placed, out_specs=P("tensor", None), check_vma=False
    )
```

time: 453 us -> 222 us (0.49)
  blocking collectives: 198 us -> 0 us
  waiting for transfers between devices: 202 us -> 103 us
  starting transfers between devices: 6.77 us -> 70.8 us
  matrix products: 29 us -> 7.38 us
  local copies, waits for them, and re-layouts: 0.78 us -> 16.2 us
  Pallas kernels: 0 us -> 13.8 us
  between operations: 13.4 us -> 0.33 us
  other arithmetic: 1.06 us -> 10.3 us
    reduce_scatter x1 -> x0, waiting for transfers between devices: 177 us -> none  [per_device(): lax.psum_scatter(jnp.dot(hidden, down_own, preferred_element_type=jnp.flo...]
    all_to_all x2 -> x0, blocking collectives: 118 us -> none  [the longest x1 71.9 us: per_device(): lax.all_to_all(gate_w, 'expert', split_axis=0, concat_axis=1, tiled=True)]
    psum x1 -> x0, blocking collectives: 80 us -> none  [per_device(): mixed = lax.psum(placed, 'expert')]
    ppermute x0 -> x33, waiting for transfers between devices: none -> 63.9 us  [tensor_move(): return lax.ppermute(value, 'tensor', pairs)]
    ppermute x0 -> x33, starting transfers between devices: none -> 53.3 us  [tensor_move(): return lax.ppermute(value, 'tensor', pairs)]
    dot_general x4 -> x6, matrix products: 29 us -> 7.38 us  [the longest x2 2.45 us: per_device(): mine = jnp.dot(hidden_mine, c, preferred_element_type=jnp.float32)]
    all_to_all x1 -> x3, waiting for transfers between devices: 24.9 us -> 38.8 us  [to_groups(): lax.all_to_all(matrix, 'expert', split_axis=0, concat_axis=1, tiled=True)[0]]
    pallas_call x0 -> x1, Pallas kernels: none -> 13.8 us  [swiglu(): pl.pallas_call(swiglu_kernel, grid=(2, count // ROW_TILE), in_specs=[pl.B...]
  transfers between devices with their start and end apart: 3 -> 36, of which waited for: 2 -> 17; matrix products, arithmetic and copies ran while one was open for 2% -> 11% of each run, Pallas kernels for 0% -> 6%
where the time goes in v1:
time: 222 us
  waiting for transfers between devices  103 us (46%)
  starting transfers between devices  70.8 us (32%)
  local copies, waits for them, and re-layouts  16.2 us (7%)
  Pallas kernels  13.8 us (6%)
  other arithmetic  10.3 us (5%)
  matrix products  7.38 us (3%)
    ppermute x33, waiting for transfers between devices, tensor_move(): return lax.ppermute(value, 'tensor', pairs)  63.9 us
    ppermute x33, starting transfers between devices, tensor_move(): return lax.ppermute(value, 'tensor', pairs)  53.3 us
    all_to_all x3, waiting for transfers between devices, to_groups(): lax.all_to_all(matrix, 'expert', split_axis=0, concat_axis=1, tiled=True)[0]  38.8 us
    all_to_all x3, starting transfers between devices, to_groups(): lax.all_to_all(matrix, 'expert', split_axis=0, concat_axis=1, tiled=True)[0]  17.5 us
    pallas_call x1, Pallas kernels, swiglu(): pl.pallas_call(swiglu_kernel, grid=(2, count // ROW_TILE), in_specs=[pl.B...  13.8 us
    unnamed x21, local copies, waits for them, and re-layouts  8.24 us
    concatenate x1, other arithmetic, per_device(): early = jnp.concatenate([gate_w, up_w, down_w[:, :EARLY]], axis=1)  6.24 us
  transfers between devices with their start and end apart: 36, of which 17 were waited for; matrix products, arithmetic and copies ran while one was open for 11% of the time, Pallas kernels for 6%

profile of v1, /device:TPU:24, one launch (start us, length us, event | category | flops | bytes accessed | tf_op | source)
XLA Modules:
  0.0 221.5 jit_solution(13401413291183915605)
XLA Ops:
  0.0 0.8 fusion.19
  1.4 1.6 collective-permute-start
  3.0 6.2 %pad_maximum_fusion = bf16[8,160,3072]{2,1,0:T(8,128)(2,1)} fusion(bf16[8,32,3072]{2,1,0:T(8,128)(2,1)S(1)} %slice-done, bf16[8,64,3072]{2,1,0:T(8,128)(2,1)} %param.10, bf16[8,64,3072]{2,1,0:T(8,128)(2,1)} %param.9), kind=kLoop, calls=%fused_computation | loop fusion | flops 23592960 | bytes 15728640 | tf_op jit(solution)/shard_map/pick/concatenate | solution.py:97
  9.3 7.1 %all-to-all-start = ((bf16[8,160,3072]{2,1,0:T(8,128)(2,1)}), bf16[8,160,3072]{2,1,0:T(8,128)(2,1)}, u32[]{:S(2)}, u32[]{:S(2)}) async-start(bf16[8,160,3072]{2,1,0:T(8,128)(2,1)} %pad_maximum_fusion), calls=%async_computation | async-start | bytes 15728640 | tf_op jit(solution)/shard_map/gate_up/all_to_all | solution.py:88
  16.4 5.9 %collective-permute-start.1 = (bf16[80,3072]{1,0:T(8,128)(2,1)S(1)}, bf16[80,3072]{1,0:T(8,128)(2,1)S(1)}, u32[]{:S(2)}, u32[]{:S(2)}) collective-permute-start(bf16[80,3072]{1,0:T(8,128)(2,1)S(1)} %pad_maximum_fusion.2), channel_id=1, source_target_pairs={{0,28},{1,29},{2,30},{3,31},{4,0},{5,1},{6,2},{7,3},{8,4},{9,5},{1... | collective-permute-start | bytes 1474568 | tf_op jit(solution)/shard_map/gate_up/ppermute | solution.py:82
  22.3 0.9 constant_dynamic-update-slice_fusion.4
  23.1 2.5 %collective-permute-start.3 = (bf16[80,3072]{1,0:T(8,128)(2,1)S(1)}, bf16[80,3072]{1,0:T(8,128)(2,1)S(1)}, u32[]{:S(2)}, u32[]{:S(2)}) collective-permute-start(bf16[80,3072]{1,0:T(8,128)(2,1)S(1)} %pad_maximum_fusion.2), channel_id=1, source_target_pairs={{0,24},{1,25},{2,26},{3,27},{4,28},{5,29},{6,30},{7,31},{8,0},{9,1... | collective-permute-start | bytes 1474568 | tf_op jit(solution)/shard_map/gate_up/ppermute | solution.py:82
  25.6 0.5 collective-permute-start.4
  26.1 18.4 %collective-permute-done.1 = bf16[80,3072]{1,0:T(8,128)(2,1)S(1)} collective-permute-done((bf16[80,3072]{1,0:T(8,128)(2,1)S(1)}, bf16[80,3072]{1,0:T(8,128)(2,1)S(1)}, u32[]{:S(2)}, u32[]{:S(2)}) %collective-permute-start.1) | collective-permute-done | bytes 491552 | tf_op jit(solution)/shard_map/gate_up/ppermute | solution.py:82
  44.5 0.9 constant_dynamic-update-slice_fusion.3
  45.4 0.9 constant_dynamic-update-slice_fusion.2
  46.2 6.5 %collective-permute-done.3 = bf16[80,3072]{1,0:T(8,128)(2,1)S(1)} collective-permute-done((bf16[80,3072]{1,0:T(8,128)(2,1)S(1)}, bf16[80,3072]{1,0:T(8,128)(2,1)S(1)}, u32[]{:S(2)}, u32[]{:S(2)}) %collective-permute-start.3) | collective-permute-done | bytes 491552 | tf_op jit(solution)/shard_map/gate_up/ppermute | solution.py:82
  52.7 0.9 constant_dynamic-update-slice_fusion.1
  53.6 0.9 constant_dynamic-update-slice_fusion
  54.5 2.8 %collective-permute-start.5 = (bf16[80,3072]{1,0:T(8,128)(2,1)S(1)}, bf16[80,3072]{1,0:T(8,128)(2,1)S(1)}, u32[]{:S(2)}, u32[]{:S(2)}) collective-permute-start(bf16[80,3072]{1,0:T(8,128)(2,1)S(1)} %collective-permute-done.3), channel_id=1, source_target_pairs={{0,28},{1,29},{2,30},{3,31},{4,0},{5,1},{6,2},{7,3},{8,4},{9,5},{1... | collective-permute-start | bytes 1474568 | tf_op jit(solution)/shard_map/gate_up/ppermute | solution.py:82
  57.2 1.2 collective-permute-start.6
  58.5 2.7 %collective-permute-start.7 = (bf16[80,1536]{1,0:T(8,128)(2,1)S(1)}, bf16[80,1536]{1,0:T(8,128)(2,1)S(1)}, u32[]{:S(2)}, u32[]{:S(2)}) collective-permute-start(bf16[80,1536]{1,0:T(8,128)(2,1)S(1)} %slice.147), channel_id=1, source_target_pairs={{0,24},{1,25},{2,26},{3,27},{4,28},{5,29},{6,30},{7,31},{8,0},{9,1... | collective-permute-start | bytes 737288 | tf_op jit(solution)/shard_map/gate_up/ppermute | solution.py:82
  61.6 1.4 slice.115
  63.0 19.1 %collective-permute-done.7 = bf16[80,1536]{1,0:T(8,128)(2,1)S(1)} collective-permute-done((bf16[80,1536]{1,0:T(8,128)(2,1)S(1)}, bf16[80,1536]{1,0:T(8,128)(2,1)S(1)}, u32[]{:S(2)}, u32[]{:S(2)}) %collective-permute-start.7) | collective-permute-done | bytes 245792 | tf_op jit(solution)/shard_map/gate_up/ppermute | solution.py:82
  82.1 0.9 collective-permute-done.8
  83.2 0.8 constant_dynamic-update-slice_fusion.9
  84.0 0.8 constant_dynamic-update-slice_fusion.8
  84.9 0.7 constant_dynamic-update-slice_fusion.7
  85.6 0.7 constant_dynamic-update-slice_fusion.15
  86.4 1.6 constant_dynamic-update-slice_fusion.6
  88.0 1.2 constant_dynamic-update-slice_fusion.5.rows_ref
  89.2 14.8 %all-to-all-done = bf16[8,160,3072]{2,1,0:T(8,128)(2,1)} async-done(((bf16[8,160,3072]{2,1,0:T(8,128)(2,1)}), bf16[8,160,3072]{2,1,0:T(8,128)(2,1)}, u32[]{:S(2)}, u32[]{:S(2)}) %all-to-all-start) | async-done | bytes 7864352 | tf_op jit(solution)/shard_map/gate_up/all_to_all | solution.py:88
  104.0 5.0 %all-to-all-start.1 = ((bf16[8,32,3072]{2,1,0:T(8,128)(2,1)}), bf16[8,32,3072]{2,1,0:T(8,128)(2,1)S(1)}, u32[]{:S(2)}, u32[]{:S(2)}) async-start(bf16[8,32,3072]{2,1,0:T(8,128)(2,1)} %slice.115), calls=%async_computation.1 | async-start | bytes 3145728 | tf_op jit(solution)/shard_map/hidden/all_to_all | solution.py:88
  109.0 13.8 %hidden.1 = bf16[1280,512]{1,0:T(8,128)(2,1)} custom-call(bf16[1280,3072]{1,0:T(8,128)(2,1)} %constant_dynamic-update-slice_fusion.5.rows_ref, bf16[8,160,3072]{2,1,0:T(8,128)(2,1)} %bitcast.3.gate_ref.up_ref, bf16[8,160,3072]{2,1,0:T(8,128)(2,1)} %bitcast.3.gate_ref.up_ref), custom_call_target="tpu_custom_call" | custom-call | flops 1000 | bytes 1000 | tf_op jit(solution)/shard_map/hidden/pallas_call | solution.py:59
  122.8 2.7 %slice.149 = bf16[8,32,3072]{2,1,0:T(8,128)(2,1)} slice(bf16[8,160,3072]{2,1,0:T(8,128)(2,1)} %bitcast.3.gate_ref.up_ref), slice={[0:8], [128:160], [0:3072]} | slice | bytes 3145728 | tf_op jit(solution)/shard_map/hidden/slice | solution.py:133
  125.5 3.9 %all-to-all-done.1 = bf16[8,32,3072]{2,1,0:T(8,128)(2,1)S(1)} async-done(((bf16[8,32,3072]{2,1,0:T(8,128)(2,1)}), bf16[8,32,3072]{2,1,0:T(8,128)(2,1)S(1)}, u32[]{:S(2)}, u32[]{:S(2)}) %all-to-all-start.1) | async-done | bytes 1572896 | tf_op jit(solution)/shard_map/hidden/all_to_all | solution.py:88
  129.3 1.8 pad_maximum_fusion.1
  131.2 1.2 convolution_convert_fusion.2
  132.5 1.2 convolution_convert_fusion.1
  133.7 0.6 collective-permute-start.22
  134.3 2.1 collective-permute-done.11
  136.4 1.2 add_convert_fusion.1
  137.7 2.0 collective-permute-start.13
  139.7 4.0 %collective-permute-start.18 = (bf16[80,1536]{1,0:T(8,128)(2,1)S(1)}, bf16[80,1536]{1,0:T(8,128)(2,1)S(1)}, u32[]{:S(2)}, u32[]{:S(2)}) collective-permute-start(bf16[80,1536]{1,0:T(8,128)(2,1)S(1)} %get-tuple-element.28), channel_id=1, source_target_pairs={{0,28},{1,29},{2,30},{3,31},{4,0},{5,1},{6,2},{7,3},{8,4},{9,5},{1... | collective-permute-start | bytes 737288 | tf_op jit(solution)/shard_map/scatter/ppermute | solution.py:82
  143.7 0.6 collective-permute-start.12
  144.4 1.2 add_convert_fusion
  145.7 2.0 collective-permute-start.24
  147.8 2.1 collective-permute-done.13
  150.1 4.5 %collective-permute-done.24 = bf16[80,1536]{1,0:T(8,128)(2,1)S(1)} collective-permute-done((bf16[80,1536]{1,0:T(8,128)(2,1)S(1)}, bf16[80,1536]{1,0:T(8,128)(2,1)S(1)}, u32[]{:S(2)}, u32[]{:S(2)}) %collective-permute-start.24) | collective-permute-done | bytes 245792 | tf_op jit(solution)/shard_map/scatter/ppermute | solution.py:82
  154.6 4.0 %collective-permute-start.25 = (bf16[80,1536]{1,0:T(8,128)(2,1)S(1)}, bf16[80,1536]{1,0:T(8,128)(2,1)S(1)}, u32[]{:S(2)}, u32[]{:S(2)}) collective-permute-start(bf16[80,1536]{1,0:T(8,128)(2,1)S(1)} %add_convert_fusion.6), channel_id=1, source_target_pairs={{0,28},{1,29},{2,30},{3,31},{4,0},{5,1},{6,2},{7,3},{8,4},{9,5},{1... | collective-permute-start | bytes 737288 | tf_op jit(solution)/shard_map/scatter/ppermute | solution.py:82
  158.6 2.5 %collective-permute-done.14 = bf16[80,1536]{1,0:T(8,128)(2,1)S(1)} collective-permute-done((bf16[80,1536]{1,0:T(8,128)(2,1)S(1)}, bf16[80,1536]{1,0:T(8,128)(2,1)S(1)}, u32[]{:S(2)}, u32[]{:S(2)}) %collective-permute-start.14) | collective-permute-done | bytes 245792 | tf_op jit(solution)/shard_map/scatter/ppermute | solution.py:82
  161.3 3.2 %collective-permute-start.19 = (bf16[80,1536]{1,0:T(8,128)(2,1)S(1)}, bf16[80,1536]{1,0:T(8,128)(2,1)S(1)}, u32[]{:S(2)}, u32[]{:S(2)}) collective-permute-start(bf16[80,1536]{1,0:T(8,128)(2,1)S(1)} %get-tuple-element.26), channel_id=1, source_target_pairs={{0,28},{1,29},{2,30},{3,31},{4,0},{5,1},{6,2},{7,3},{8,4},{9,5},{1... | collective-permute-start | bytes 737288 | tf_op jit(solution)/shard_map/scatter/ppermute | solution.py:82
  164.6 3.3 %collective-permute-start.26 = (bf16[80,1536]{1,0:T(8,128)(2,1)S(1)}, bf16[80,1536]{1,0:T(8,128)(2,1)S(1)}, u32[]{:S(2)}, u32[]{:S(2)}) collective-permute-start(bf16[80,1536]{1,0:T(8,128)(2,1)S(1)} %get-tuple-element.31), channel_id=1, source_target_pairs={{0,28},{1,29},{2,30},{3,31},{4,0},{5,1},{6,2},{7,3},{8,4},{9,5},{1... | collective-permute-start | bytes 737288 | tf_op jit(solution)/shard_map/scatter/ppermute | solution.py:82
  167.9 0.7 collective-permute-done.15
  168.7 2.2 %collective-permute-done.19 = bf16[80,1536]{1,0:T(8,128)(2,1)S(1)} collective-permute-done((bf16[80,1536]{1,0:T(8,128)(2,1)S(1)}, bf16[80,1536]{1,0:T(8,128)(2,1)S(1)}, u32[]{:S(2)}, u32[]{:S(2)}) %collective-permute-start.19) | collective-permute-done | bytes 245792 | tf_op jit(solution)/shard_map/scatter/ppermute | solution.py:82
  171.2 2.7 %collective-permute-start.17 = (bf16[40,1536]{1,0:T(8,128)(2,1)S(1)}, bf16[40,1536]{1,0:T(8,128)(2,1)S(1)}, u32[]{:S(2)}, u32[]{:S(2)}) collective-permute-start(bf16[40,1536]{1,0:T(8,128)(2,1)S(1)} %get-tuple-element.46), channel_id=1, source_target_pairs={{0,6},{1,7},{2,4},{3,5},{4,10},{5,11},{6,8},{7,9},{8,14},{9,15},{1... | collective-permute-start | bytes 368648 | tf_op jit(solution)/shard_map/scatter/ppermute | solution.py:82
  173.8 3.6 %collective-permute-start.20 = (bf16[40,1536]{1,0:T(8,128)(2,1)S(1)}, bf16[40,1536]{1,0:T(8,128)(2,1)S(1)}, u32[]{:S(2)}, u32[]{:S(2)}) collective-permute-start(bf16[40,1536]{1,0:T(8,128)(2,1)S(1)} %get-tuple-element.47), channel_id=1, source_target_pairs={{0,28},{1,29},{2,30},{3,31},{4,0},{5,1},{6,2},{7,3},{8,4},{9,5},{1... | collective-permute-start | bytes 368648 | tf_op jit(solution)/shard_map/scatter/ppermute | solution.py:82
  177.5 0.5 collective-permute-start.21
  178.2 1.1 collective-permute-start.23
  179.2 1.8 collective-permute-start.27
  181.1 1.5 collective-permute-start.28
  182.6 1.1 collective-permute-start.31
  183.7 1.2 collective-permute-done.21
  184.9 3.4 %collective-permute-start.32 = (bf16[40,1536]{1,0:T(8,128)(2,1)S(1)}, bf16[40,1536]{1,0:T(8,128)(2,1)S(1)}, u32[]{:S(2)}, u32[]{:S(2)}) collective-permute-start(bf16[40,1536]{1,0:T(8,128)(2,1)S(1)} %get-tuple-element.52), channel_id=1, source_target_pairs={{0,6},{1,7},{2,4},{3,5},{4,10},{5,11},{6,8},{7,9},{8,14},{9,15},{1... | collective-permute-start | bytes 368648 | tf_op jit(solution)/shard_map/scatter/ppermute | solution.py:82
  188.7 3.2 %collective-permute-done.32 = bf16[40,1536]{1,0:T(8,128)(2,1)S(1)} collective-permute-done((bf16[40,1536]{1,0:T(8,128)(2,1)S(1)}, bf16[40,1536]{1,0:T(8,128)(2,1)S(1)}, u32[]{:S(2)}, u32[]{:S(2)}) %collective-permute-start.32) | collective-permute-done | bytes 122912 | tf_op jit(solution)/shard_map/scatter/ppermute | solution.py:82
  192.1 1.5 broadcast_in_dim.20
  193.6 5.4 %all-to-all-start.2 = ((bf16[8,40,3072]{2,1,0:T(8,128)(2,1)}), bf16[8,40,3072]{2,1,0:T(8,128)(2,1)S(1)}, u32[]{:S(2)}, u32[]{:S(2)}) async-start(bf16[8,40,3072]{2,1,0:T(8,128)(2,1)} %broadcast_in_dim.20), calls=%async_computation.2 | async-start | bytes 3932160 | tf_op jit(solution)/shard_map/mix/all_to_all | solution.py:88
  199.0 20.2 %all-to-all-done.2 = bf16[8,40,3072]{2,1,0:T(8,128)(2,1)S(1)} async-done(((bf16[8,40,3072]{2,1,0:T(8,128)(2,1)}), bf16[8,40,3072]{2,1,0:T(8,128)(2,1)S(1)}, u32[]{:S(2)}, u32[]{:S(2)}) %all-to-all-start.2) | async-done | bytes 1966112 | tf_op jit(solution)/shard_map/mix/all_to_all | solution.py:88
  219.2 2.3 %fusion = bf16[128,3072]{1,0:T(8,128)(2,1)} fusion(bf16[8,40,3072]{2,1,0:T(8,128)(2,1)S(1)} %all-to-all-done.2, f32[8,128]{1,0:T(8,128)S(1)} %select_reduce_fusion, s32[8,128]{1,0:T(8,128)S(1)} %broadcast_add_fusion, pred[8,128]{1,0:T(8,128)(4,1)S(1)} %fusion.19), kind=kOutput, calls=%fused_computation.4 | convolution fusion | flops 1510465536 | bytes 2761728 | tf_op jit(solution)/shard_map/mix/dot_general | solution.py:175
  (73 shorter events, 3.2 us)
Async XLA Ops:
  0.0 1.2 copy-start
  0.0 3.0 %slice-start = ((bf16[8,64,3072]{2,1,0:T(8,128)(2,1)}), bf16[8,32,3072]{2,1,0:T(8,128)(2,1)S(1)}, s32[]{:S(2)}) async-start(bf16[8,64,3072]{2,1,0:T(8,128)(2,1)} %param.11), calls=%async_computation.3 | async-start | bytes 3145728 | tf_op jit(solution)/shard_map/pick/slice | solution.py:97
  1.4 7.8 %collective-permute-start = (bf16[40,3072]{1,0:T(8,128)(2,1)S(1)}, bf16[40,3072]{1,0:T(8,128)(2,1)S(1)}, u32[]{:S(2)}, u32[]{:S(2)}) collective-permute-start(bf16[40,3072]{1,0:T(8,128)(2,1)S(1)} %convolution_convert_fusion), channel_id=1, source_target_pairs={{0,2},{1,3},{2,0},{3,1},{4,6},{5,7},{6,4},{7,5},{8,10},{9,11},{10,... | collective-permute-start | bytes 737288 | tf_op jit(solution)/shard_map/pick/ppermute | solution.py:82
  9.3 94.7 %all-to-all-start = ((bf16[8,160,3072]{2,1,0:T(8,128)(2,1)}), bf16[8,160,3072]{2,1,0:T(8,128)(2,1)}, u32[]{:S(2)}, u32[]{:S(2)}) async-start(bf16[8,160,3072]{2,1,0:T(8,128)(2,1)} %pad_maximum_fusion), calls=%async_computation | async-start | bytes 15728640 | tf_op jit(solution)/shard_map/gate_up/all_to_all | solution.py:88
  16.4 28.1 %collective-permute-start.1 = (bf16[80,3072]{1,0:T(8,128)(2,1)S(1)}, bf16[80,3072]{1,0:T(8,128)(2,1)S(1)}, u32[]{:S(2)}, u32[]{:S(2)}) collective-permute-start(bf16[80,3072]{1,0:T(8,128)(2,1)S(1)} %pad_maximum_fusion.2), channel_id=1, source_target_pairs={{0,28},{1,29},{2,30},{3,31},{4,0},{5,1},{6,2},{7,3},{8,4},{9,5},{1... | collective-permute-start | bytes 1474568 | tf_op jit(solution)/shard_map/gate_up/ppermute | solution.py:82
  22.3 23.1 %collective-permute-start.2 = (bf16[80,3072]{1,0:T(8,128)(2,1)S(1)}, bf16[80,3072]{1,0:T(8,128)(2,1)S(1)}, u32[]{:S(2)}, u32[]{:S(2)}) collective-permute-start(bf16[80,3072]{1,0:T(8,128)(2,1)S(1)} %pad_maximum_fusion.2), channel_id=1, source_target_pairs={{0,4},{1,5},{2,6},{3,7},{4,8},{5,9},{6,10},{7,11},{8,12},{9,13},{1... | collective-permute-start | bytes 1474568 | tf_op jit(solution)/shard_map/gate_up/ppermute | solution.py:82
  23.1 29.6 %collective-permute-start.3 = (bf16[80,3072]{1,0:T(8,128)(2,1)S(1)}, bf16[80,3072]{1,0:T(8,128)(2,1)S(1)}, u32[]{:S(2)}, u32[]{:S(2)}) collective-permute-start(bf16[80,3072]{1,0:T(8,128)(2,1)S(1)} %pad_maximum_fusion.2), channel_id=1, source_target_pairs={{0,24},{1,25},{2,26},{3,27},{4,28},{5,29},{6,30},{7,31},{8,0},{9,1... | collective-permute-start | bytes 1474568 | tf_op jit(solution)/shard_map/gate_up/ppermute | solution.py:82
  25.6 28.0 %collective-permute-start.4 = (bf16[80,3072]{1,0:T(8,128)(2,1)S(1)}, bf16[80,3072]{1,0:T(8,128)(2,1)S(1)}, u32[]{:S(2)}, u32[]{:S(2)}) collective-permute-start(bf16[80,3072]{1,0:T(8,128)(2,1)S(1)} %pad_maximum_fusion.2), channel_id=1, source_target_pairs={{0,8},{1,9},{2,10},{3,11},{4,12},{5,13},{6,14},{7,15},{8,16},{9,17... | collective-permute-start | bytes 1474568 | tf_op jit(solution)/shard_map/gate_up/ppermute | solution.py:82
  45.3 16.2 %copy-start.2 = (bf16[8,64,3072]{2,1,0:T(8,128)(2,1)S(1)}, bf16[8,64,3072]{2,1,0:T(8,128)(2,1)}, u32[]{:S(2)}) copy-start(bf16[8,64,3072]{2,1,0:T(8,128)(2,1)} %param.11) | copy-start | bytes 9437188
  54.5 31.9 %collective-permute-start.9 = (bf16[400,3072]{1,0:T(8,128)(2,1)S(1)}, bf16[400,3072]{1,0:T(8,128)(2,1)S(1)}, u32[]{:S(2)}, u32[]{:S(2)}) collective-permute-start(bf16[400,3072]{1,0:T(8,128)(2,1)S(1)} %get-tuple-element.35), channel_id=1, source_target_pairs={{0,1},{1,0},{2,3},{3,2},{4,5},{5,4},{6,7},{7,6},{8,9},{9,8},{10,11... | collective-permute-start | bytes 7372808 | tf_op jit(solution)/shard_map/gate_up/ppermute | solution.py:82
  54.5 28.5 %collective-permute-start.5 = (bf16[80,3072]{1,0:T(8,128)(2,1)S(1)}, bf16[80,3072]{1,0:T(8,128)(2,1)S(1)}, u32[]{:S(2)}, u32[]{:S(2)}) collective-permute-start(bf16[80,3072]{1,0:T(8,128)(2,1)S(1)} %collective-permute-done.3), channel_id=1, source_target_pairs={{0,28},{1,29},{2,30},{3,31},{4,0},{5,1},{6,2},{7,3},{8,4},{9,5},{1... | collective-permute-start | bytes 1474568 | tf_op jit(solution)/shard_map/gate_up/ppermute | solution.py:82
  57.2 25.7 %collective-permute-start.6 = (bf16[80,3072]{1,0:T(8,128)(2,1)S(1)}, bf16[80,3072]{1,0:T(8,128)(2,1)S(1)}, u32[]{:S(2)}, u32[]{:S(2)}) collective-permute-start(bf16[80,3072]{1,0:T(8,128)(2,1)S(1)} %collective-permute-done.4), channel_id=1, source_target_pairs={{0,4},{1,5},{2,6},{3,7},{4,8},{5,9},{6,10},{7,11},{8,12},{9,13},{1... | collective-permute-start | bytes 1474568 | tf_op jit(solution)/shard_map/gate_up/ppermute | solution.py:82
  58.5 23.6 %collective-permute-start.7 = (bf16[80,1536]{1,0:T(8,128)(2,1)S(1)}, bf16[80,1536]{1,0:T(8,128)(2,1)S(1)}, u32[]{:S(2)}, u32[]{:S(2)}) collective-permute-start(bf16[80,1536]{1,0:T(8,128)(2,1)S(1)} %slice.147), channel_id=1, source_target_pairs={{0,24},{1,25},{2,26},{3,27},{4,28},{5,29},{6,30},{7,31},{8,0},{9,1... | collective-permute-start | bytes 737288 | tf_op jit(solution)/shard_map/gate_up/ppermute | solution.py:82
  61.2 21.7 %collective-permute-start.8 = (bf16[80,1536]{1,0:T(8,128)(2,1)S(1)}, bf16[80,1536]{1,0:T(8,128)(2,1)S(1)}, u32[]{:S(2)}, u32[]{:S(2)}) collective-permute-start(bf16[80,1536]{1,0:T(8,128)(2,1)S(1)} %slice.148), channel_id=1, source_target_pairs={{0,8},{1,9},{2,10},{3,11},{4,12},{5,13},{6,14},{7,15},{8,16},{9,17... | collective-permute-start | bytes 737288 | tf_op jit(solution)/shard_map/gate_up/ppermute | solution.py:82
  83.1 4.8 %collective-permute-start.10 = (bf16[240,3072]{1,0:T(8,128)(2,1)S(1)}, bf16[240,3072]{1,0:T(8,128)(2,1)S(1)}, u32[]{:S(2)}, u32[]{:S(2)}) collective-permute-start(bf16[240,3072]{1,0:T(8,128)(2,1)S(1)} %maximum_maximum_fusion), channel_id=1, source_target_pairs={{0,1},{1,0},{2,3},{3,2},{4,5},{5,4},{6,7},{7,6},{8,9},{9,8},{10,11... | collective-permute-start | bytes 4423688 | tf_op jit(solution)/shard_map/gate_up/ppermute | solution.py:82
  104.0 25.4 %all-to-all-start.1 = ((bf16[8,32,3072]{2,1,0:T(8,128)(2,1)}), bf16[8,32,3072]{2,1,0:T(8,128)(2,1)S(1)}, u32[]{:S(2)}, u32[]{:S(2)}) async-start(bf16[8,32,3072]{2,1,0:T(8,128)(2,1)} %slice.115), calls=%async_computation.1 | async-start | bytes 3145728 | tf_op jit(solution)/shard_map/hidden/all_to_all | solution.py:88
  129.3 1.8 copy-start.3
  132.4 4.1 %collective-permute-start.11 = (bf16[640,1536]{1,0:T(8,128)(2,1)S(1)}, bf16[640,1536]{1,0:T(8,128)(2,1)S(1)}, u32[]{:S(2)}, u32[]{:S(2)}) collective-permute-start(bf16[640,1536]{1,0:T(8,128)(2,1)S(1)} %convolution_convert_fusion.2), channel_id=1, source_target_pairs={{0,1},{1,0},{2,3},{3,2},{4,5},{5,4},{6,7},{7,6},{8,9},{9,8},{10,11... | collective-permute-start | bytes 5898248 | tf_op jit(solution)/shard_map/down/ppermute | solution.py:82
  133.7 10.7 %collective-permute-start.22 = (bf16[640,1536]{1,0:T(8,128)(2,1)S(1)}, bf16[640,1536]{1,0:T(8,128)(2,1)S(1)}, u32[]{:S(2)}, u32[]{:S(2)}) collective-permute-start(bf16[640,1536]{1,0:T(8,128)(2,1)S(1)} %convolution_convert_fusion.1), channel_id=1, source_target_pairs={{0,1},{1,0},{2,3},{3,2},{4,5},{5,4},{6,7},{7,6},{8,9},{9,8},{10,11... | collective-permute-start | bytes 5898248 | tf_op jit(solution)/shard_map/down/ppermute | solution.py:82
  137.7 12.2 %collective-permute-start.13 = (bf16[80,1536]{1,0:T(8,128)(2,1)S(1)}, bf16[80,1536]{1,0:T(8,128)(2,1)S(1)}, u32[]{:S(2)}, u32[]{:S(2)}) collective-permute-start(bf16[80,1536]{1,0:T(8,128)(2,1)S(1)} %get-tuple-element.27), channel_id=1, source_target_pairs={{0,4},{1,5},{2,6},{3,7},{4,8},{5,9},{6,10},{7,11},{8,12},{9,13},{1... | collective-permute-start | bytes 737288 | tf_op jit(solution)/shard_map/scatter/ppermute | solution.py:82
  139.7 18.9 %collective-permute-start.18 = (bf16[80,1536]{1,0:T(8,128)(2,1)S(1)}, bf16[80,1536]{1,0:T(8,128)(2,1)S(1)}, u32[]{:S(2)}, u32[]{:S(2)}) collective-permute-start(bf16[80,1536]{1,0:T(8,128)(2,1)S(1)} %get-tuple-element.28), channel_id=1, source_target_pairs={{0,28},{1,29},{2,30},{3,31},{4,0},{5,1},{6,2},{7,3},{8,4},{9,5},{1... | collective-permute-start | bytes 737288 | tf_op jit(solution)/shard_map/scatter/ppermute | solution.py:82
  143.7 34.4 %collective-permute-start.12 = (bf16[40,1536]{1,0:T(8,128)(2,1)S(1)}, bf16[40,1536]{1,0:T(8,128)(2,1)S(1)}, u32[]{:S(2)}, u32[]{:S(2)}) collective-permute-start(bf16[40,1536]{1,0:T(8,128)(2,1)S(1)} %slice.153), channel_id=1, source_target_pairs={{0,2},{1,3},{2,0},{3,1},{4,6},{5,7},{6,4},{7,5},{8,10},{9,11},{10,... | collective-permute-start | bytes 368648 | tf_op jit(solution)/shard_map/scatter/ppermute | solution.py:82
  145.7 8.9 %collective-permute-start.24 = (bf16[80,1536]{1,0:T(8,128)(2,1)S(1)}, bf16[80,1536]{1,0:T(8,128)(2,1)S(1)}, u32[]{:S(2)}, u32[]{:S(2)}) collective-permute-start(bf16[80,1536]{1,0:T(8,128)(2,1)S(1)} %get-tuple-element.33), channel_id=1, source_target_pairs={{0,28},{1,29},{2,30},{3,31},{4,0},{5,1},{6,2},{7,3},{8,4},{9,5},{1... | collective-permute-start | bytes 737288 | tf_op jit(solution)/shard_map/scatter/ppermute | solution.py:82
  147.7 16.8 %collective-permute-start.29 = (bf16[80,1536]{1,0:T(8,128)(2,1)S(1)}, bf16[80,1536]{1,0:T(8,128)(2,1)S(1)}, u32[]{:S(2)}, u32[]{:S(2)}) collective-permute-start(bf16[80,1536]{1,0:T(8,128)(2,1)S(1)} %get-tuple-element.34), channel_id=1, source_target_pairs={{0,4},{1,5},{2,6},{3,7},{4,8},{5,9},{6,10},{7,11},{8,12},{9,13},{1... | collective-permute-start | bytes 737288 | tf_op jit(solution)/shard_map/scatter/ppermute | solution.py:82
  150.0 11.1 %collective-permute-start.14 = (bf16[80,1536]{1,0:T(8,128)(2,1)S(1)}, bf16[80,1536]{1,0:T(8,128)(2,1)S(1)}, u32[]{:S(2)}, u32[]{:S(2)}) collective-permute-start(bf16[80,1536]{1,0:T(8,128)(2,1)S(1)} %add_convert_fusion.11), channel_id=1, source_target_pairs={{0,4},{1,5},{2,6},{3,7},{4,8},{5,9},{6,10},{7,11},{8,12},{9,13},{1... | collective-permute-start | bytes 737288 | tf_op jit(solution)/shard_map/scatter/ppermute | solution.py:82
  154.6 9.9 %collective-permute-start.25 = (bf16[80,1536]{1,0:T(8,128)(2,1)S(1)}, bf16[80,1536]{1,0:T(8,128)(2,1)S(1)}, u32[]{:S(2)}, u32[]{:S(2)}) collective-permute-start(bf16[80,1536]{1,0:T(8,128)(2,1)S(1)} %add_convert_fusion.6), channel_id=1, source_target_pairs={{0,28},{1,29},{2,30},{3,31},{4,0},{5,1},{6,2},{7,3},{8,4},{9,5},{1... | collective-permute-start | bytes 737288 | tf_op jit(solution)/shard_map/scatter/ppermute | solution.py:82
  161.2 7.5 %collective-permute-start.15 = (bf16[80,1536]{1,0:T(8,128)(2,1)S(1)}, bf16[80,1536]{1,0:T(8,128)(2,1)S(1)}, u32[]{:S(2)}, u32[]{:S(2)}) collective-permute-start(bf16[80,1536]{1,0:T(8,128)(2,1)S(1)} %get-tuple-element.25), channel_id=1, source_target_pairs={{0,4},{1,5},{2,6},{3,7},{4,8},{5,9},{6,10},{7,11},{8,12},{9,13},{1... | collective-permute-start | bytes 737288 | tf_op jit(solution)/shard_map/scatter/ppermute | solution.py:82
  161.3 9.6 %collective-permute-start.19 = (bf16[80,1536]{1,0:T(8,128)(2,1)S(1)}, bf16[80,1536]{1,0:T(8,128)(2,1)S(1)}, u32[]{:S(2)}, u32[]{:S(2)}) collective-permute-start(bf16[80,1536]{1,0:T(8,128)(2,1)S(1)} %get-tuple-element.26), channel_id=1, source_target_pairs={{0,28},{1,29},{2,30},{3,31},{4,0},{5,1},{6,2},{7,3},{8,4},{9,5},{1... | collective-permute-start | bytes 737288 | tf_op jit(solution)/shard_map/scatter/ppermute | solution.py:82
  164.6 9.2 %collective-permute-start.26 = (bf16[80,1536]{1,0:T(8,128)(2,1)S(1)}, bf16[80,1536]{1,0:T(8,128)(2,1)S(1)}, u32[]{:S(2)}, u32[]{:S(2)}) collective-permute-start(bf16[80,1536]{1,0:T(8,128)(2,1)S(1)} %get-tuple-element.31), channel_id=1, source_target_pairs={{0,28},{1,29},{2,30},{3,31},{4,0},{5,1},{6,2},{7,3},{8,4},{9,5},{1... | collective-permute-start | bytes 737288 | tf_op jit(solution)/shard_map/scatter/ppermute | solution.py:82
  167.9 9.6 %collective-permute-start.30 = (bf16[80,1536]{1,0:T(8,128)(2,1)S(1)}, bf16[80,1536]{1,0:T(8,128)(2,1)S(1)}, u32[]{:S(2)}, u32[]{:S(2)}) collective-permute-start(bf16[80,1536]{1,0:T(8,128)(2,1)S(1)} %get-tuple-element.32), channel_id=1, source_target_pairs={{0,4},{1,5},{2,6},{3,7},{4,8},{5,9},{6,10},{7,11},{8,12},{9,13},{1... | collective-permute-start | bytes 737288 | tf_op jit(solution)/shard_map/scatter/ppermute | solution.py:82
  171.1 8.2 %collective-permute-start.16 = (bf16[40,1536]{1,0:T(8,128)(2,1)S(1)}, bf16[40,1536]{1,0:T(8,128)(2,1)S(1)}, u32[]{:S(2)}, u32[]{:S(2)}) collective-permute-start(bf16[40,1536]{1,0:T(8,128)(2,1)S(1)} %get-tuple-element.45), channel_id=1, source_target_pairs={{0,4},{1,5},{2,6},{3,7},{4,8},{5,9},{6,10},{7,11},{8,12},{9,13},{1... | collective-permute-start | bytes 368648 | tf_op jit(solution)/shard_map/scatter/ppermute | solution.py:82
  171.2 10.0 %collective-permute-start.17 = (bf16[40,1536]{1,0:T(8,128)(2,1)S(1)}, bf16[40,1536]{1,0:T(8,128)(2,1)S(1)}, u32[]{:S(2)}, u32[]{:S(2)}) collective-permute-start(bf16[40,1536]{1,0:T(8,128)(2,1)S(1)} %get-tuple-element.46), channel_id=1, source_target_pairs={{0,6},{1,7},{2,4},{3,5},{4,10},{5,11},{6,8},{7,9},{8,14},{9,15},{1... | collective-permute-start | bytes 368648 | tf_op jit(solution)/shard_map/scatter/ppermute | solution.py:82
  173.8 8.8 %collective-permute-start.20 = (bf16[40,1536]{1,0:T(8,128)(2,1)S(1)}, bf16[40,1536]{1,0:T(8,128)(2,1)S(1)}, u32[]{:S(2)}, u32[]{:S(2)}) collective-permute-start(bf16[40,1536]{1,0:T(8,128)(2,1)S(1)} %get-tuple-element.47), channel_id=1, source_target_pairs={{0,28},{1,29},{2,30},{3,31},{4,0},{5,1},{6,2},{7,3},{8,4},{9,5},{1... | collective-permute-start | bytes 368648 | tf_op jit(solution)/shard_map/scatter/ppermute | solution.py:82
  177.5 7.4 %collective-permute-start.21 = (bf16[40,1536]{1,0:T(8,128)(2,1)S(1)}, bf16[40,1536]{1,0:T(8,128)(2,1)S(1)}, u32[]{:S(2)}, u32[]{:S(2)}) collective-permute-start(bf16[40,1536]{1,0:T(8,128)(2,1)S(1)} %get-tuple-element.48), channel_id=1, source_target_pairs={{0,30},{1,31},{2,28},{3,29},{4,2},{5,3},{6,0},{7,1},{8,6},{9,7},{1... | collective-permute-start | bytes 368648 | tf_op jit(solution)/shard_map/scatter/ppermute | solution.py:82
  178.2 10.2 %collective-permute-start.23 = (bf16[40,1536]{1,0:T(8,128)(2,1)S(1)}, bf16[40,1536]{1,0:T(8,128)(2,1)S(1)}, u32[]{:S(2)}, u32[]{:S(2)}) collective-permute-start(bf16[40,1536]{1,0:T(8,128)(2,1)S(1)} %slice.166), channel_id=1, source_target_pairs={{0,2},{1,3},{2,0},{3,1},{4,6},{5,7},{6,4},{7,5},{8,10},{9,11},{10,... | collective-permute-start | bytes 368648 | tf_op jit(solution)/shard_map/scatter/ppermute | solution.py:82
  179.2 9.2 %collective-permute-start.27 = (bf16[40,1536]{1,0:T(8,128)(2,1)S(1)}, bf16[40,1536]{1,0:T(8,128)(2,1)S(1)}, u32[]{:S(2)}, u32[]{:S(2)}) collective-permute-start(bf16[40,1536]{1,0:T(8,128)(2,1)S(1)} %get-tuple-element.49), channel_id=1, source_target_pairs={{0,28},{1,29},{2,30},{3,31},{4,0},{5,1},{6,2},{7,3},{8,4},{9,5},{1... | collective-permute-start | bytes 368648 | tf_op jit(solution)/shard_map/scatter/ppermute | solution.py:82
  181.1 7.3 %collective-permute-start.28 = (bf16[40,1536]{1,0:T(8,128)(2,1)S(1)}, bf16[40,1536]{1,0:T(8,128)(2,1)S(1)}, u32[]{:S(2)}, u32[]{:S(2)}) collective-permute-start(bf16[40,1536]{1,0:T(8,128)(2,1)S(1)} %get-tuple-element.50), channel_id=1, source_target_pairs={{0,30},{1,31},{2,28},{3,29},{4,2},{5,3},{6,0},{7,1},{8,6},{9,7},{1... | collective-permute-start | bytes 368648 | tf_op jit(solution)/shard_map/scatter/ppermute | solution.py:82
  182.6 6.1 %collective-permute-start.31 = (bf16[40,1536]{1,0:T(8,128)(2,1)S(1)}, bf16[40,1536]{1,0:T(8,128)(2,1)S(1)}, u32[]{:S(2)}, u32[]{:S(2)}) collective-permute-start(bf16[40,1536]{1,0:T(8,128)(2,1)S(1)} %get-tuple-element.51), channel_id=1, source_target_pairs={{0,4},{1,5},{2,6},{3,7},{4,8},{5,9},{6,10},{7,11},{8,12},{9,13},{1... | collective-permute-start | bytes 368648 | tf_op jit(solution)/shard_map/scatter/ppermute | solution.py:82
  184.9 7.0 %collective-permute-start.32 = (bf16[40,1536]{1,0:T(8,128)(2,1)S(1)}, bf16[40,1536]{1,0:T(8,128)(2,1)S(1)}, u32[]{:S(2)}, u32[]{:S(2)}) collective-permute-start(bf16[40,1536]{1,0:T(8,128)(2,1)S(1)} %get-tuple-element.52), channel_id=1, source_target_pairs={{0,6},{1,7},{2,4},{3,5},{4,10},{5,11},{6,8},{7,9},{8,14},{9,15},{1... | collective-permute-start | bytes 368648 | tf_op jit(solution)/shard_map/scatter/ppermute | solution.py:82
  192.0 7.0 %copy-start.4 = (s32[128,2]{0,1:T(2,128)S(1)}, s32[128,2]{0,1:T(2,128)}, u32[]{:S(2)}) copy-start(s32[128,2]{0,1:T(2,128)} %param.7) | copy-start | bytes 3076
  192.0 7.0 %copy-start.5 = (f32[128,2]{0,1:T(2,128)S(1)}, f32[128,2]{0,1:T(2,128)}, u32[]{:S(2)}) copy-start(f32[128,2]{0,1:T(2,128)} %param.8) | copy-start | bytes 3076
  192.1 29.5 %copy-start.1 = (bf16[128,3072]{1,0:T(8,128)(2,1)S(1)}, bf16[128,3072]{1,0:T(8,128)(2,1)}, u32[]{:S(2)}) copy-start(bf16[128,3072]{1,0:T(8,128)(2,1)} %param.6) | copy-start | bytes 2359300
  193.6 25.6 %all-to-all-start.2 = ((bf16[8,40,3072]{2,1,0:T(8,128)(2,1)}), bf16[8,40,3072]{2,1,0:T(8,128)(2,1)S(1)}, u32[]{:S(2)}, u32[]{:S(2)}) async-start(bf16[8,40,3072]{2,1,0:T(8,128)(2,1)} %broadcast_in_dim.20), calls=%async_computation.2 | async-start | bytes 3932160 | tf_op jit(solution)/shard_map/mix/all_to_all | solution.py:88

commit v2 on v1

--- a/solution.py
+++ b/solution.py
@@ -5,7 +5,6 @@
 from jax.experimental.pallas import tpu as pltpu
 from jax.sharding import PartitionSpec as P
 
-CHUNKS = (1536, 1536)
 EARLY = 32
 ROW_TILE = 640
 
@@ -128,45 +127,39 @@
         early = early.reshape(expert_count, -1, width)
         hidden = swiglu(rows, early, depth)
 
-        late, hidden = lax.optimization_barrier((late, hidden))
+        hidden = hidden.reshape(2, 8, 2, capacity, -1)
+        mine, others = ([part[:, n].reshape(8 * capacity, -1) for n in (0, 1)] for part in hidden)
+        late, mine, others = lax.optimization_barrier((late, mine, others))
         late = late.reshape(expert_count, -1, width)
         down_own = jnp.concatenate([early[:, 2 * depth :], late], axis=1).reshape(-1, width)
 
-    own_rows = rows.shape[0] // 2
-    edges = [sum(CHUNKS[:n]) for n in range(len(CHUNKS) + 1)]
-    columns = [down_own[:, a:b] for a, b in zip(edges[:-1], edges[1:])]
     with jax.named_scope("down"):
         theirs = [
-            jnp.dot(hidden[own_rows:], c, preferred_element_type=jnp.float32).astype(bf16)
-            for c in columns
+            jnp.dot(rows, down_own, preferred_element_type=jnp.float32).astype(bf16)
+            for rows in others
         ]
         received = [tensor_move(t, CORE) for t in theirs]
-        hidden_mine, _ = lax.optimization_barrier((hidden[:own_rows], theirs))
+        mine, _ = lax.optimization_barrier((mine, theirs))
         totals = []
-        for c, got in zip(columns, received):
-            mine = jnp.dot(hidden_mine, c, preferred_element_type=jnp.float32)
-            totals.append((mine + got.astype(jnp.float32)).astype(bf16))
+        for rows, got in zip(mine, received):
+            here = jnp.dot(rows, down_own, preferred_element_type=jnp.float32)
+            totals.append((here + got.astype(jnp.float32)).astype(bf16))
 
-    def chains(total, longer):
-        size = total.shape[0] // 8
-        part = {k: total[i * size : (i + 1) * size] for i, k in enumerate(order)}
-        moving = {longer: tensor_move(part[4], along_z(longer))}
-        for k in (3, 2):
-            for way in (longer, -longer):
-                here = part[way * k]
-                if way in moving:
-                    here = add(moving[way], here).astype(bf16)
-                moving[way] = tensor_move(here, along_z(way))
-        summed = part[0][:capacity].astype(jnp.float32)
-        summed = add(summed, tensor_move(part[0][capacity:], X_LO))
-        for way in (longer, -longer):
-            here = add(moving[way], part[way]).astype(bf16)
-            summed = add(summed, tensor_move(here[:capacity], along_z(way)))
-            summed = add(summed, tensor_move(here[capacity:], along_z(way, 2)))
-        return summed.astype(bf16)
+    def chains(total, longer, flip):
+        part = {k: total[i * capacity : (i + 1) * capacity] for i, k in enumerate(order)}
+        stay = tensor_move(part[0], X_LO) if flip else part[0]
+        far = tensor_move(part[4], along_z(longer))
+        near = tensor_move(part[-3 * longer], along_z(-longer))
+        far = tensor_move(add(far, part[3 * longer]).astype(bf16), along_z(longer))
+        near = tensor_move(add(near, part[-2 * longer]).astype(bf16), along_z(-longer))
+        far = tensor_move(add(far, part[2 * longer]).astype(bf16), along_z(longer))
+        near = tensor_move(add(near, part[-longer]).astype(bf16), along_z(-longer, flip))
+        far = tensor_move(add(far, part[longer]).astype(bf16), along_z(longer, flip))
+        return add(stay, near) + far.astype(jnp.float32)
 
     with jax.named_scope("scatter"):
-        outs = [chains(t, 1 if n % 2 == 0 else -1) for n, t in enumerate(totals)]
+        summed = chains(totals[1], -1, 2) + chains(totals[0], 1, 0)
+        outs = [summed.astype(bf16)]
 
     with jax.named_scope("mix"):
         scaled = onehot * weight[:, None, :]

time: 222 us -> 220 us (level)
  starting transfers between devices: 70.8 us -> 61.9 us
  waiting for transfers between devices: 103 us -> 109 us
    ppermute x33 -> x28, starting transfers between devices: 53.3 us -> 44.5 us  [tensor_move(): return lax.ppermute(value, 'tensor', pairs)]
    ppermute x33 -> x28, waiting for transfers between devices: 63.9 us -> 68.4 us  [tensor_move(): return lax.ppermute(value, 'tensor', pairs)]
    unnamed x21 -> x23, local copies, waits for them, and re-layouts: 8.24 us -> 8.24 us
  transfers between devices with their start and end apart: 36 -> 31, of which waited for: 17 -> 17; matrix products, arithmetic and copies ran while one was open for 11% -> 12% of each run, Pallas kernels for 6% -> 6%
where the time goes in v2:
time: 220 us; the launch traced here: 219 us
  waiting for transfers between devices  109 us (50%)
  starting transfers between devices  61.9 us (28%)
  local copies, waits for them, and re-layouts  17.1 us (8%)
  Pallas kernels  13.8 us (6%)
  other arithmetic  10.1 us (5%)
  matrix products  7.59 us (3%)
    ppermute x28, waiting for transfers between devices, tensor_move(): return lax.ppermute(value, 'tensor', pairs)  68.4 us
    ppermute x28, starting transfers between devices, tensor_move(): return lax.ppermute(value, 'tensor', pairs)  44.5 us
    all_to_all x3, waiting for transfers between devices, to_groups(): lax.all_to_all(matrix, 'expert', split_axis=0, concat_axis=1, tiled=True)[0]  40.2 us
    all_to_all x3, starting transfers between devices, to_groups(): lax.all_to_all(matrix, 'expert', split_axis=0, concat_axis=1, tiled=True)[0]  17.4 us
    pallas_call x1, Pallas kernels, swiglu(): pl.pallas_call(swiglu_kernel, grid=(2, count // ROW_TILE), in_specs=[pl.B...  13.8 us
    unnamed x23, local copies, waits for them, and re-layouts  8.24 us
    concatenate x1, other arithmetic, per_device(): early = jnp.concatenate([gate_w, up_w, down_w[:, :EARLY]], axis=1)  6.25 us
  transfers between devices with their start and end apart: 31, of which 17 were waited for; matrix products, arithmetic and copies ran while one was open for 12% of the time, Pallas kernels for 6%

profile of v2, /device:TPU:24, one launch (start us, length us, event | category | flops | bytes accessed | tf_op | source)
XLA Modules:
  0.0 219.5 jit_solution(12625532371879484459)
XLA Ops:
  0.0 0.8 fusion.7
  0.8 0.3 reduce_window_sum.11
  1.2 0.2 convolution_convert_fusion.2
  1.4 1.6 collective-permute-start
  3.0 6.2 %pad_maximum_fusion = bf16[8,160,3072]{2,1,0:T(8,128)(2,1)} fusion(bf16[8,32,3072]{2,1,0:T(8,128)(2,1)S(1)} %slice-done, bf16[8,64,3072]{2,1,0:T(8,128)(2,1)} %param.10, bf16[8,64,3072]{2,1,0:T(8,128)(2,1)} %param.9), kind=kLoop, calls=%fused_computation | loop fusion | flops 23592960 | bytes 15728640 | tf_op jit(solution)/shard_map/pick/concatenate | solution.py:96
  9.3 7.1 %all-to-all-start = ((bf16[8,160,3072]{2,1,0:T(8,128)(2,1)}), bf16[8,160,3072]{2,1,0:T(8,128)(2,1)}, u32[]{:S(2)}, u32[]{:S(2)}) async-start(bf16[8,160,3072]{2,1,0:T(8,128)(2,1)} %pad_maximum_fusion), calls=%async_computation | async-start | bytes 15728640 | tf_op jit(solution)/shard_map/gate_up/all_to_all | solution.py:87
  16.4 5.9 %collective-permute-start.1 = (bf16[80,3072]{1,0:T(8,128)(2,1)S(1)}, bf16[80,3072]{1,0:T(8,128)(2,1)S(1)}, u32[]{:S(2)}, u32[]{:S(2)}) collective-permute-start(bf16[80,3072]{1,0:T(8,128)(2,1)S(1)} %pad_maximum_fusion.2), channel_id=1, source_target_pairs={{0,28},{1,29},{2,30},{3,31},{4,0},{5,1},{6,2},{7,3},{8,4},{9,5},{1... | collective-permute-start | bytes 1474568 | tf_op jit(solution)/shard_map/gate_up/ppermute | solution.py:81
  22.3 0.9 constant_dynamic-update-slice_fusion.4
  23.1 2.5 %collective-permute-start.3 = (bf16[80,3072]{1,0:T(8,128)(2,1)S(1)}, bf16[80,3072]{1,0:T(8,128)(2,1)S(1)}, u32[]{:S(2)}, u32[]{:S(2)}) collective-permute-start(bf16[80,3072]{1,0:T(8,128)(2,1)S(1)} %pad_maximum_fusion.2), channel_id=1, source_target_pairs={{0,24},{1,25},{2,26},{3,27},{4,28},{5,29},{6,30},{7,31},{8,0},{9,1... | collective-permute-start | bytes 1474568 | tf_op jit(solution)/shard_map/gate_up/ppermute | solution.py:81
  25.6 0.5 collective-permute-start.4
  26.1 18.4 %collective-permute-done.1 = bf16[80,3072]{1,0:T(8,128)(2,1)S(1)} collective-permute-done((bf16[80,3072]{1,0:T(8,128)(2,1)S(1)}, bf16[80,3072]{1,0:T(8,128)(2,1)S(1)}, u32[]{:S(2)}, u32[]{:S(2)}) %collective-permute-start.1) | collective-permute-done | bytes 491552 | tf_op jit(solution)/shard_map/gate_up/ppermute | solution.py:81
  44.5 0.9 constant_dynamic-update-slice_fusion.3
  45.4 0.8 constant_dynamic-update-slice_fusion.2
  46.2 6.5 %collective-permute-done.3 = bf16[80,3072]{1,0:T(8,128)(2,1)S(1)} collective-permute-done((bf16[80,3072]{1,0:T(8,128)(2,1)S(1)}, bf16[80,3072]{1,0:T(8,128)(2,1)S(1)}, u32[]{:S(2)}, u32[]{:S(2)}) %collective-permute-start.3) | collective-permute-done | bytes 491552 | tf_op jit(solution)/shard_map/gate_up/ppermute | solution.py:81
  52.7 0.9 constant_dynamic-update-slice_fusion.1
  53.6 0.9 constant_dynamic-update-slice_fusion
  54.5 2.8 %collective-permute-start.5 = (bf16[80,3072]{1,0:T(8,128)(2,1)S(1)}, bf16[80,3072]{1,0:T(8,128)(2,1)S(1)}, u32[]{:S(2)}, u32[]{:S(2)}) collective-permute-start(bf16[80,3072]{1,0:T(8,128)(2,1)S(1)} %collective-permute-done.3), channel_id=1, source_target_pairs={{0,28},{1,29},{2,30},{3,31},{4,0},{5,1},{6,2},{7,3},{8,4},{9,5},{1... | collective-permute-start | bytes 1474568 | tf_op jit(solution)/shard_map/gate_up/ppermute | solution.py:81
  57.3 1.2 collective-permute-start.6
  58.5 2.7 %collective-permute-start.7 = (bf16[80,1536]{1,0:T(8,128)(2,1)S(1)}, bf16[80,1536]{1,0:T(8,128)(2,1)S(1)}, u32[]{:S(2)}, u32[]{:S(2)}) collective-permute-start(bf16[80,1536]{1,0:T(8,128)(2,1)S(1)} %slice.102), channel_id=1, source_target_pairs={{0,24},{1,25},{2,26},{3,27},{4,28},{5,29},{6,30},{7,31},{8,0},{9,1... | collective-permute-start | bytes 737288 | tf_op jit(solution)/shard_map/gate_up/ppermute | solution.py:81
  61.2 0.4 collective-permute-start.8
  61.6 1.4 slice.80
  63.0 19.1 %collective-permute-done.7 = bf16[80,1536]{1,0:T(8,128)(2,1)S(1)} collective-permute-done((bf16[80,1536]{1,0:T(8,128)(2,1)S(1)}, bf16[80,1536]{1,0:T(8,128)(2,1)S(1)}, u32[]{:S(2)}, u32[]{:S(2)}) %collective-permute-start.7) | collective-permute-done | bytes 245792 | tf_op jit(solution)/shard_map/gate_up/ppermute | solution.py:81
  82.1 0.9 collective-permute-done.8
  83.2 0.8 constant_dynamic-update-slice_fusion.9
  84.1 0.8 constant_dynamic-update-slice_fusion.8
  84.9 0.7 constant_dynamic-update-slice_fusion.7
  85.6 0.7 constant_dynamic-update-slice_fusion.15
  86.4 1.6 constant_dynamic-update-slice_fusion.6
  88.0 1.2 constant_dynamic-update-slice_fusion.5.rows_ref
  89.2 14.8 %all-to-all-done = bf16[8,160,3072]{2,1,0:T(8,128)(2,1)} async-done(((bf16[8,160,3072]{2,1,0:T(8,128)(2,1)}), bf16[8,160,3072]{2,1,0:T(8,128)(2,1)}, u32[]{:S(2)}, u32[]{:S(2)}) %all-to-all-start) | async-done | bytes 7864352 | tf_op jit(solution)/shard_map/gate_up/all_to_all | solution.py:87
  104.0 5.0 %all-to-all-start.1 = ((bf16[8,32,3072]{2,1,0:T(8,128)(2,1)}), bf16[8,32,3072]{2,1,0:T(8,128)(2,1)S(1)}, u32[]{:S(2)}, u32[]{:S(2)}) async-start(bf16[8,32,3072]{2,1,0:T(8,128)(2,1)} %slice.80), calls=%async_computation.1 | async-start | bytes 3145728 | tf_op jit(solution)/shard_map/hidden/all_to_all | solution.py:87
  109.0 13.8 %hidden.1 = bf16[1280,512]{1,0:T(8,128)(2,1)} custom-call(bf16[1280,3072]{1,0:T(8,128)(2,1)} %constant_dynamic-update-slice_fusion.5.rows_ref, bf16[8,160,3072]{2,1,0:T(8,128)(2,1)} %bitcast.3.gate_ref.up_ref, bf16[8,160,3072]{2,1,0:T(8,128)(2,1)} %bitcast.3.gate_ref.up_ref), custom_call_target="tpu_custom_call" | custom-call | flops 1000 | bytes 1000 | tf_op jit(solution)/shard_map/hidden/pallas_call | solution.py:58
  122.8 2.8 %slice.108 = bf16[8,32,3072]{2,1,0:T(8,128)(2,1)} slice(bf16[8,160,3072]{2,1,0:T(8,128)(2,1)} %bitcast.3.gate_ref.up_ref), slice={[0:8], [128:160], [0:3072]} | slice | bytes 3145728 | tf_op jit(solution)/shard_map/hidden/slice | solution.py:134
  125.7 0.8 fusion.14
  126.5 2.9 %all-to-all-done.1 = bf16[8,32,3072]{2,1,0:T(8,128)(2,1)S(1)} async-done(((bf16[8,32,3072]{2,1,0:T(8,128)(2,1)}), bf16[8,32,3072]{2,1,0:T(8,128)(2,1)S(1)}, u32[]{:S(2)}, u32[]{:S(2)}) %all-to-all-start.1) | async-done | bytes 1572896 | tf_op jit(solution)/shard_map/hidden/all_to_all | solution.py:87
  129.4 1.7 pad_maximum_fusion.1
  131.1 1.2 convolution_convert_fusion
  132.5 1.2 convolution_convert_fusion.1
  133.7 0.6 collective-permute-start.20
  134.3 2.1 collective-permute-done.11
  136.4 1.3 add_convert_fusion.1
  137.8 5.9 %collective-permute-start.16 = (bf16[40,3072]{1,0:T(8,128)(2,1)S(1)}, bf16[40,3072]{1,0:T(8,128)(2,1)S(1)}, u32[]{:S(2)}, u32[]{:S(2)}) collective-permute-start(bf16[40,3072]{1,0:T(8,128)(2,1)S(1)} %get-tuple-element.32), channel_id=1, source_target_pairs={{0,28},{1,29},{2,30},{3,31},{4,0},{5,1},{6,2},{7,3},{8,4},{9,5},{1... | collective-permute-start | bytes 737288 | tf_op jit(solution)/shard_map/scatter/ppermute | solution.py:81
  143.7 0.6 collective-permute-start.12
  144.3 1.3 add_convert_fusion
  145.7 3.3 %collective-permute-start.21 = (bf16[40,3072]{1,0:T(8,128)(2,1)S(1)}, bf16[40,3072]{1,0:T(8,128)(2,1)S(1)}, u32[]{:S(2)}, u32[]{:S(2)}) collective-permute-start(bf16[40,3072]{1,0:T(8,128)(2,1)S(1)} %get-tuple-element.42), channel_id=1, source_target_pairs={{0,28},{1,29},{2,30},{3,31},{4,0},{5,1},{6,2},{7,3},{8,4},{9,5},{1... | collective-permute-start | bytes 737288 | tf_op jit(solution)/shard_map/scatter/ppermute | solution.py:81
  149.1 0.8 collective-permute-done.16
  150.0 3.8 %collective-permute-start.17 = (bf16[40,3072]{1,0:T(8,128)(2,1)S(1)}, bf16[40,3072]{1,0:T(8,128)(2,1)S(1)}, u32[]{:S(2)}, u32[]{:S(2)}) collective-permute-start(bf16[40,3072]{1,0:T(8,128)(2,1)S(1)} %add_convert_fusion.10), channel_id=1, source_target_pairs={{0,28},{1,29},{2,30},{3,31},{4,0},{5,1},{6,2},{7,3},{8,4},{9,5},{1... | collective-permute-start | bytes 737288 | tf_op jit(solution)/shard_map/scatter/ppermute | solution.py:81
  153.7 4.2 %collective-permute-done.24 = bf16[40,3072]{1,0:T(8,128)(2,1)S(1)} collective-permute-done((bf16[40,3072]{1,0:T(8,128)(2,1)S(1)}, bf16[40,3072]{1,0:T(8,128)(2,1)S(1)}, u32[]{:S(2)}, u32[]{:S(2)}) %collective-permute-start.24) | collective-permute-done | bytes 245792 | tf_op jit(solution)/shard_map/scatter/ppermute | solution.py:81
  158.0 0.3 collective-permute-start.25
  158.3 1.5 collective-permute-done.17
  160.0 3.8 %collective-permute-start.18 = (bf16[40,3072]{1,0:T(8,128)(2,1)S(1)}, bf16[40,3072]{1,0:T(8,128)(2,1)S(1)}, u32[]{:S(2)}, u32[]{:S(2)}) collective-permute-start(bf16[40,3072]{1,0:T(8,128)(2,1)S(1)} %get-tuple-element.37), channel_id=1, source_target_pairs={{0,28},{1,29},{2,30},{3,31},{4,0},{5,1},{6,2},{7,3},{8,4},{9,5},{1... | collective-permute-start | bytes 737288 | tf_op jit(solution)/shard_map/scatter/ppermute | solution.py:81
  163.7 4.6 %collective-permute-done.25 = bf16[40,3072]{1,0:T(8,128)(2,1)S(1)} collective-permute-done((bf16[40,3072]{1,0:T(8,128)(2,1)S(1)}, bf16[40,3072]{1,0:T(8,128)(2,1)S(1)}, u32[]{:S(2)}, u32[]{:S(2)}) %collective-permute-start.25) | collective-permute-done | bytes 245792 | tf_op jit(solution)/shard_map/scatter/ppermute | solution.py:81
  168.6 2.0 collective-permute-start.26
  170.6 3.0 %collective-permute-done.14 = bf16[40,3072]{1,0:T(8,128)(2,1)S(1)} collective-permute-done((bf16[40,3072]{1,0:T(8,128)(2,1)S(1)}, bf16[40,3072]{1,0:T(8,128)(2,1)S(1)}, u32[]{:S(2)}, u32[]{:S(2)}) %collective-permute-start.14) | collective-permute-done | bytes 245792 | tf_op jit(solution)/shard_map/scatter/ppermute | solution.py:81
  173.8 4.1 %collective-permute-start.19 = (bf16[40,3072]{1,0:T(8,128)(2,1)S(1)}, bf16[40,3072]{1,0:T(8,128)(2,1)S(1)}, u32[]{:S(2)}, u32[]{:S(2)}) collective-permute-start(bf16[40,3072]{1,0:T(8,128)(2,1)S(1)} %get-tuple-element.35), channel_id=1, source_target_pairs={{0,30},{1,31},{2,28},{3,29},{4,2},{5,3},{6,0},{7,1},{8,6},{9,7},{1... | collective-permute-start | bytes 737288 | tf_op jit(solution)/shard_map/scatter/ppermute | solution.py:81
  178.0 0.9 collective-permute-done.26
  179.1 2.0 collective-permute-start.27
  181.1 3.7 %collective-permute-done.15 = bf16[40,3072]{1,0:T(8,128)(2,1)S(1)} collective-permute-done((bf16[40,3072]{1,0:T(8,128)(2,1)S(1)}, bf16[40,3072]{1,0:T(8,128)(2,1)S(1)}, u32[]{:S(2)}, u32[]{:S(2)}) %collective-permute-start.15) | collective-permute-done | bytes 245792 | tf_op jit(solution)/shard_map/scatter/ppermute | solution.py:81
  184.8 0.6 collective-permute-done.23
  185.5 1.9 collective-permute-done.27
  187.6 1.5 broadcast_in_dim.20
  189.2 5.4 %all-to-all-start.2 = ((bf16[8,40,3072]{2,1,0:T(8,128)(2,1)}), bf16[8,40,3072]{2,1,0:T(8,128)(2,1)S(1)}, u32[]{:S(2)}, u32[]{:S(2)}) async-start(bf16[8,40,3072]{2,1,0:T(8,128)(2,1)} %broadcast_in_dim.20), calls=%async_computation.2 | async-start | bytes 3932160 | tf_op jit(solution)/shard_map/mix/all_to_all | solution.py:87
  194.5 22.6 %all-to-all-done.2 = bf16[8,40,3072]{2,1,0:T(8,128)(2,1)S(1)} async-done(((bf16[8,40,3072]{2,1,0:T(8,128)(2,1)}), bf16[8,40,3072]{2,1,0:T(8,128)(2,1)S(1)}, u32[]{:S(2)}, u32[]{:S(2)}) %all-to-all-start.2) | async-done | bytes 1966112 | tf_op jit(solution)/shard_map/mix/all_to_all | solution.py:87
  217.1 2.3 %fusion = bf16[128,3072]{1,0:T(8,128)(2,1)} fusion(bf16[8,40,3072]{2,1,0:T(8,128)(2,1)S(1)} %all-to-all-done.2, f32[8,128]{1,0:T(8,128)S(1)} %select_reduce_fusion, s32[8,128]{1,0:T(8,128)S(1)} %broadcast_add_fusion, pred[8,128]{1,0:T(8,128)(4,1)S(1)} %fusion.7), kind=kOutput, calls=%fused_computation.6 | convolution fusion | flops 1510465536 | bytes 2761728 | tf_op jit(solution)/shard_map/mix/dot_general | solution.py:168
  (59 shorter events, 2.0 us)
Async XLA Ops:
  0.0 1.2 copy-start
  0.0 3.0 %slice-start = ((bf16[8,64,3072]{2,1,0:T(8,128)(2,1)}), bf16[8,32,3072]{2,1,0:T(8,128)(2,1)S(1)}, s32[]{:S(2)}) async-start(bf16[8,64,3072]{2,1,0:T(8,128)(2,1)} %param.11), calls=%async_computation.3 | async-start | bytes 3145728 | tf_op jit(solution)/shard_map/pick/slice | solution.py:96
  1.4 7.8 %collective-permute-start = (bf16[40,3072]{1,0:T(8,128)(2,1)S(1)}, bf16[40,3072]{1,0:T(8,128)(2,1)S(1)}, u32[]{:S(2)}, u32[]{:S(2)}) collective-permute-start(bf16[40,3072]{1,0:T(8,128)(2,1)S(1)} %convolution_convert_fusion.2), channel_id=1, source_target_pairs={{0,2},{1,3},{2,0},{3,1},{4,6},{5,7},{6,4},{7,5},{8,10},{9,11},{10,... | collective-permute-start | bytes 737288 | tf_op jit(solution)/shard_map/pick/ppermute | solution.py:81
  9.3 94.7 %all-to-all-start = ((bf16[8,160,3072]{2,1,0:T(8,128)(2,1)}), bf16[8,160,3072]{2,1,0:T(8,128)(2,1)}, u32[]{:S(2)}, u32[]{:S(2)}) async-start(bf16[8,160,3072]{2,1,0:T(8,128)(2,1)} %pad_maximum_fusion), calls=%async_computation | async-start | bytes 15728640 | tf_op jit(solution)/shard_map/gate_up/all_to_all | solution.py:87
  16.4 28.1 %collective-permute-start.1 = (bf16[80,3072]{1,0:T(8,128)(2,1)S(1)}, bf16[80,3072]{1,0:T(8,128)(2,1)S(1)}, u32[]{:S(2)}, u32[]{:S(2)}) collective-permute-start(bf16[80,3072]{1,0:T(8,128)(2,1)S(1)} %pad_maximum_fusion.2), channel_id=1, source_target_pairs={{0,28},{1,29},{2,30},{3,31},{4,0},{5,1},{6,2},{7,3},{8,4},{9,5},{1... | collective-permute-start | bytes 1474568 | tf_op jit(solution)/shard_map/gate_up/ppermute | solution.py:81
  22.3 23.1 %collective-permute-start.2 = (bf16[80,3072]{1,0:T(8,128)(2,1)S(1)}, bf16[80,3072]{1,0:T(8,128)(2,1)S(1)}, u32[]{:S(2)}, u32[]{:S(2)}) collective-permute-start(bf16[80,3072]{1,0:T(8,128)(2,1)S(1)} %pad_maximum_fusion.2), channel_id=1, source_target_pairs={{0,4},{1,5},{2,6},{3,7},{4,8},{5,9},{6,10},{7,11},{8,12},{9,13},{1... | collective-permute-start | bytes 1474568 | tf_op jit(solution)/shard_map/gate_up/ppermute | solution.py:81
  23.1 29.6 %collective-permute-start.3 = (bf16[80,3072]{1,0:T(8,128)(2,1)S(1)}, bf16[80,3072]{1,0:T(8,128)(2,1)S(1)}, u32[]{:S(2)}, u32[]{:S(2)}) collective-permute-start(bf16[80,3072]{1,0:T(8,128)(2,1)S(1)} %pad_maximum_fusion.2), channel_id=1, source_target_pairs={{0,24},{1,25},{2,26},{3,27},{4,28},{5,29},{6,30},{7,31},{8,0},{9,1... | collective-permute-start | bytes 1474568 | tf_op jit(solution)/shard_map/gate_up/ppermute | solution.py:81
  25.6 28.0 %collective-permute-start.4 = (bf16[80,3072]{1,0:T(8,128)(2,1)S(1)}, bf16[80,3072]{1,0:T(8,128)(2,1)S(1)}, u32[]{:S(2)}, u32[]{:S(2)}) collective-permute-start(bf16[80,3072]{1,0:T(8,128)(2,1)S(1)} %pad_maximum_fusion.2), channel_id=1, source_target_pairs={{0,8},{1,9},{2,10},{3,11},{4,12},{5,13},{6,14},{7,15},{8,16},{9,17... | collective-permute-start | bytes 1474568 | tf_op jit(solution)/shard_map/gate_up/ppermute | solution.py:81
  44.5 17.1 %copy-start.2 = (bf16[8,64,3072]{2,1,0:T(8,128)(2,1)S(1)}, bf16[8,64,3072]{2,1,0:T(8,128)(2,1)}, u32[]{:S(2)}) copy-start(bf16[8,64,3072]{2,1,0:T(8,128)(2,1)} %param.11) | copy-start | bytes 9437188
  54.5 31.9 %collective-permute-start.9 = (bf16[400,3072]{1,0:T(8,128)(2,1)S(1)}, bf16[400,3072]{1,0:T(8,128)(2,1)S(1)}, u32[]{:S(2)}, u32[]{:S(2)}) collective-permute-start(bf16[400,3072]{1,0:T(8,128)(2,1)S(1)} %get-tuple-element.50), channel_id=1, source_target_pairs={{0,1},{1,0},{2,3},{3,2},{4,5},{5,4},{6,7},{7,6},{8,9},{9,8},{10,11... | collective-permute-start | bytes 7372808 | tf_op jit(solution)/shard_map/gate_up/ppermute | solution.py:81
  54.5 28.5 %collective-permute-start.5 = (bf16[80,3072]{1,0:T(8,128)(2,1)S(1)}, bf16[80,3072]{1,0:T(8,128)(2,1)S(1)}, u32[]{:S(2)}, u32[]{:S(2)}) collective-permute-start(bf16[80,3072]{1,0:T(8,128)(2,1)S(1)} %collective-permute-done.3), channel_id=1, source_target_pairs={{0,28},{1,29},{2,30},{3,31},{4,0},{5,1},{6,2},{7,3},{8,4},{9,5},{1... | collective-permute-start | bytes 1474568 | tf_op jit(solution)/shard_map/gate_up/ppermute | solution.py:81
  57.3 25.7 %collective-permute-start.6 = (bf16[80,3072]{1,0:T(8,128)(2,1)S(1)}, bf16[80,3072]{1,0:T(8,128)(2,1)S(1)}, u32[]{:S(2)}, u32[]{:S(2)}) collective-permute-start(bf16[80,3072]{1,0:T(8,128)(2,1)S(1)} %collective-permute-done.4), channel_id=1, source_target_pairs={{0,4},{1,5},{2,6},{3,7},{4,8},{5,9},{6,10},{7,11},{8,12},{9,13},{1... | collective-permute-start | bytes 1474568 | tf_op jit(solution)/shard_map/gate_up/ppermute | solution.py:81
  58.5 23.6 %collective-permute-start.7 = (bf16[80,1536]{1,0:T(8,128)(2,1)S(1)}, bf16[80,1536]{1,0:T(8,128)(2,1)S(1)}, u32[]{:S(2)}, u32[]{:S(2)}) collective-permute-start(bf16[80,1536]{1,0:T(8,128)(2,1)S(1)} %slice.102), channel_id=1, source_target_pairs={{0,24},{1,25},{2,26},{3,27},{4,28},{5,29},{6,30},{7,31},{8,0},{9,1... | collective-permute-start | bytes 737288 | tf_op jit(solution)/shard_map/gate_up/ppermute | solution.py:81
  61.2 21.7 %collective-permute-start.8 = (bf16[80,1536]{1,0:T(8,128)(2,1)S(1)}, bf16[80,1536]{1,0:T(8,128)(2,1)S(1)}, u32[]{:S(2)}, u32[]{:S(2)}) collective-permute-start(bf16[80,1536]{1,0:T(8,128)(2,1)S(1)} %slice.103), channel_id=1, source_target_pairs={{0,8},{1,9},{2,10},{3,11},{4,12},{5,13},{6,14},{7,15},{8,16},{9,17... | collective-permute-start | bytes 737288 | tf_op jit(solution)/shard_map/gate_up/ppermute | solution.py:81
  83.1 4.9 %collective-permute-start.10 = (bf16[240,3072]{1,0:T(8,128)(2,1)S(1)}, bf16[240,3072]{1,0:T(8,128)(2,1)S(1)}, u32[]{:S(2)}, u32[]{:S(2)}) collective-permute-start(bf16[240,3072]{1,0:T(8,128)(2,1)S(1)} %maximum_maximum_fusion), channel_id=1, source_target_pairs={{0,1},{1,0},{2,3},{3,2},{4,5},{5,4},{6,7},{7,6},{8,9},{9,8},{10,11... | collective-permute-start | bytes 4423688 | tf_op jit(solution)/shard_map/gate_up/ppermute | solution.py:81
  104.0 25.4 %all-to-all-start.1 = ((bf16[8,32,3072]{2,1,0:T(8,128)(2,1)}), bf16[8,32,3072]{2,1,0:T(8,128)(2,1)S(1)}, u32[]{:S(2)}, u32[]{:S(2)}) async-start(bf16[8,32,3072]{2,1,0:T(8,128)(2,1)} %slice.80), calls=%async_computation.1 | async-start | bytes 3145728 | tf_op jit(solution)/shard_map/hidden/all_to_all | solution.py:87
  122.8 2.8 %copy-start.3 = (bf16[1280,512]{1,0:T(8,128)(2,1)S(1)}, bf16[1280,512]{1,0:T(8,128)(2,1)}, u32[]{:S(2)}) copy-start(bf16[1280,512]{1,0:T(8,128)(2,1)} %hidden.1) | copy-start | bytes 3932164
  129.4 1.8 copy-start.4
  132.4 4.1 %collective-permute-start.11 = (bf16[320,3072]{1,0:T(8,128)(2,1)S(1)}, bf16[320,3072]{1,0:T(8,128)(2,1)S(1)}, u32[]{:S(2)}, u32[]{:S(2)}) collective-permute-start(bf16[320,3072]{1,0:T(8,128)(2,1)S(1)} %convolution_convert_fusion), channel_id=1, source_target_pairs={{0,1},{1,0},{2,3},{3,2},{4,5},{5,4},{6,7},{7,6},{8,9},{9,8},{10,11... | collective-permute-start | bytes 5898248 | tf_op jit(solution)/shard_map/down/ppermute | solution.py:81
  133.7 10.6 %collective-permute-start.20 = (bf16[320,3072]{1,0:T(8,128)(2,1)S(1)}, bf16[320,3072]{1,0:T(8,128)(2,1)S(1)}, u32[]{:S(2)}, u32[]{:S(2)}) collective-permute-start(bf16[320,3072]{1,0:T(8,128)(2,1)S(1)} %convolution_convert_fusion.1), channel_id=1, source_target_pairs={{0,1},{1,0},{2,3},{3,2},{4,5},{5,4},{6,7},{7,6},{8,9},{9,8},{10,11... | collective-permute-start | bytes 5898248 | tf_op jit(solution)/shard_map/down/ppermute | solution.py:81
  137.8 12.1 %collective-permute-start.16 = (bf16[40,3072]{1,0:T(8,128)(2,1)S(1)}, bf16[40,3072]{1,0:T(8,128)(2,1)S(1)}, u32[]{:S(2)}, u32[]{:S(2)}) collective-permute-start(bf16[40,3072]{1,0:T(8,128)(2,1)S(1)} %get-tuple-element.32), channel_id=1, source_target_pairs={{0,28},{1,29},{2,30},{3,31},{4,0},{5,1},{6,2},{7,3},{8,4},{9,5},{1... | collective-permute-start | bytes 737288 | tf_op jit(solution)/shard_map/scatter/ppermute | solution.py:81
  143.7 14.6 %collective-permute-start.13 = (bf16[40,3072]{1,0:T(8,128)(2,1)S(1)}, bf16[40,3072]{1,0:T(8,128)(2,1)S(1)}, u32[]{:S(2)}, u32[]{:S(2)}) collective-permute-start(bf16[40,3072]{1,0:T(8,128)(2,1)S(1)} %get-tuple-element.33), channel_id=1, source_target_pairs={{0,4},{1,5},{2,6},{3,7},{4,8},{5,9},{6,10},{7,11},{8,12},{9,13},{1... | collective-permute-start | bytes 737288 | tf_op jit(solution)/shard_map/scatter/ppermute | solution.py:81
  143.7 37.4 %collective-permute-start.12 = (bf16[40,3072]{1,0:T(8,128)(2,1)S(1)}, bf16[40,3072]{1,0:T(8,128)(2,1)S(1)}, u32[]{:S(2)}, u32[]{:S(2)}) collective-permute-start(bf16[40,3072]{1,0:T(8,128)(2,1)S(1)} %get-tuple-element.31), channel_id=1, source_target_pairs={{0,2},{1,3},{2,0},{3,1},{4,6},{5,7},{6,4},{7,5},{8,10},{9,11},{10,... | collective-permute-start | bytes 737288 | tf_op jit(solution)/shard_map/scatter/ppermute | solution.py:81
  145.7 12.2 %collective-permute-start.24 = (bf16[40,3072]{1,0:T(8,128)(2,1)S(1)}, bf16[40,3072]{1,0:T(8,128)(2,1)S(1)}, u32[]{:S(2)}, u32[]{:S(2)}) collective-permute-start(bf16[40,3072]{1,0:T(8,128)(2,1)S(1)} %get-tuple-element.43), channel_id=1, source_target_pairs={{0,4},{1,5},{2,6},{3,7},{4,8},{5,9},{6,10},{7,11},{8,12},{9,13},{1... | collective-permute-start | bytes 737288 | tf_op jit(solution)/shard_map/scatter/ppermute | solution.py:81
  145.7 18.0 %collective-permute-start.21 = (bf16[40,3072]{1,0:T(8,128)(2,1)S(1)}, bf16[40,3072]{1,0:T(8,128)(2,1)S(1)}, u32[]{:S(2)}, u32[]{:S(2)}) collective-permute-start(bf16[40,3072]{1,0:T(8,128)(2,1)S(1)} %get-tuple-element.42), channel_id=1, source_target_pairs={{0,28},{1,29},{2,30},{3,31},{4,0},{5,1},{6,2},{7,3},{8,4},{9,5},{1... | collective-permute-start | bytes 737288 | tf_op jit(solution)/shard_map/scatter/ppermute | solution.py:81
  150.0 9.8 %collective-permute-start.17 = (bf16[40,3072]{1,0:T(8,128)(2,1)S(1)}, bf16[40,3072]{1,0:T(8,128)(2,1)S(1)}, u32[]{:S(2)}, u32[]{:S(2)}) collective-permute-start(bf16[40,3072]{1,0:T(8,128)(2,1)S(1)} %add_convert_fusion.10), channel_id=1, source_target_pairs={{0,28},{1,29},{2,30},{3,31},{4,0},{5,1},{6,2},{7,3},{8,4},{9,5},{1... | collective-permute-start | bytes 737288 | tf_op jit(solution)/shard_map/scatter/ppermute | solution.py:81
  158.0 10.4 %collective-permute-start.25 = (bf16[40,3072]{1,0:T(8,128)(2,1)S(1)}, bf16[40,3072]{1,0:T(8,128)(2,1)S(1)}, u32[]{:S(2)}, u32[]{:S(2)}) collective-permute-start(bf16[40,3072]{1,0:T(8,128)(2,1)S(1)} %add_convert_fusion.5), channel_id=1, source_target_pairs={{0,4},{1,5},{2,6},{3,7},{4,8},{5,9},{6,10},{7,11},{8,12},{9,13},{1... | collective-permute-start | bytes 737288 | tf_op jit(solution)/shard_map/scatter/ppermute | solution.py:81
  159.9 13.8 %collective-permute-start.14 = (bf16[40,3072]{1,0:T(8,128)(2,1)S(1)}, bf16[40,3072]{1,0:T(8,128)(2,1)S(1)}, u32[]{:S(2)}, u32[]{:S(2)}) collective-permute-start(bf16[40,3072]{1,0:T(8,128)(2,1)S(1)} %get-tuple-element.36), channel_id=1, source_target_pairs={{0,4},{1,5},{2,6},{3,7},{4,8},{5,9},{6,10},{7,11},{8,12},{9,13},{1... | collective-permute-start | bytes 737288 | tf_op jit(solution)/shard_map/scatter/ppermute | solution.py:81
  160.0 13.7 %collective-permute-start.18 = (bf16[40,3072]{1,0:T(8,128)(2,1)S(1)}, bf16[40,3072]{1,0:T(8,128)(2,1)S(1)}, u32[]{:S(2)}, u32[]{:S(2)}) collective-permute-start(bf16[40,3072]{1,0:T(8,128)(2,1)S(1)} %get-tuple-element.37), channel_id=1, source_target_pairs={{0,28},{1,29},{2,30},{3,31},{4,0},{5,1},{6,2},{7,3},{8,4},{9,5},{1... | collective-permute-start | bytes 737288 | tf_op jit(solution)/shard_map/scatter/ppermute | solution.py:81
  168.5 9.5 %collective-permute-start.22 = (bf16[40,3072]{1,0:T(8,128)(2,1)S(1)}, bf16[40,3072]{1,0:T(8,128)(2,1)S(1)}, u32[]{:S(2)}, u32[]{:S(2)}) collective-permute-start(bf16[40,3072]{1,0:T(8,128)(2,1)S(1)} %get-tuple-element.40), channel_id=1, source_target_pairs={{0,28},{1,29},{2,30},{3,31},{4,0},{5,1},{6,2},{7,3},{8,4},{9,5},{1... | collective-permute-start | bytes 737288 | tf_op jit(solution)/shard_map/scatter/ppermute | solution.py:81
  168.6 10.3 %collective-permute-start.26 = (bf16[40,3072]{1,0:T(8,128)(2,1)S(1)}, bf16[40,3072]{1,0:T(8,128)(2,1)S(1)}, u32[]{:S(2)}, u32[]{:S(2)}) collective-permute-start(bf16[40,3072]{1,0:T(8,128)(2,1)S(1)} %get-tuple-element.41), channel_id=1, source_target_pairs={{0,4},{1,5},{2,6},{3,7},{4,8},{5,9},{6,10},{7,11},{8,12},{9,13},{1... | collective-permute-start | bytes 737288 | tf_op jit(solution)/shard_map/scatter/ppermute | solution.py:81
  173.8 11.1 %collective-permute-start.15 = (bf16[40,3072]{1,0:T(8,128)(2,1)S(1)}, bf16[40,3072]{1,0:T(8,128)(2,1)S(1)}, u32[]{:S(2)}, u32[]{:S(2)}) collective-permute-start(bf16[40,3072]{1,0:T(8,128)(2,1)S(1)} %get-tuple-element.34), channel_id=1, source_target_pairs={{0,6},{1,7},{2,4},{3,5},{4,10},{5,11},{6,8},{7,9},{8,14},{9,15},{1... | collective-permute-start | bytes 737288 | tf_op jit(solution)/shard_map/scatter/ppermute | solution.py:81
  173.8 11.0 %collective-permute-start.19 = (bf16[40,3072]{1,0:T(8,128)(2,1)S(1)}, bf16[40,3072]{1,0:T(8,128)(2,1)S(1)}, u32[]{:S(2)}, u32[]{:S(2)}) collective-permute-start(bf16[40,3072]{1,0:T(8,128)(2,1)S(1)} %get-tuple-element.35), channel_id=1, source_target_pairs={{0,30},{1,31},{2,28},{3,29},{4,2},{5,3},{6,0},{7,1},{8,6},{9,7},{1... | collective-permute-start | bytes 737288 | tf_op jit(solution)/shard_map/scatter/ppermute | solution.py:81
  179.0 6.4 %collective-permute-start.23 = (bf16[40,3072]{1,0:T(8,128)(2,1)S(1)}, bf16[40,3072]{1,0:T(8,128)(2,1)S(1)}, u32[]{:S(2)}, u32[]{:S(2)}) collective-permute-start(bf16[40,3072]{1,0:T(8,128)(2,1)S(1)} %get-tuple-element.38), channel_id=1, source_target_pairs={{0,28},{1,29},{2,30},{3,31},{4,0},{5,1},{6,2},{7,3},{8,4},{9,5},{1... | collective-permute-start | bytes 737288 | tf_op jit(solution)/shard_map/scatter/ppermute | solution.py:81
  179.1 8.3 %collective-permute-start.27 = (bf16[40,3072]{1,0:T(8,128)(2,1)S(1)}, bf16[40,3072]{1,0:T(8,128)(2,1)S(1)}, u32[]{:S(2)}, u32[]{:S(2)}) collective-permute-start(bf16[40,3072]{1,0:T(8,128)(2,1)S(1)} %get-tuple-element.39), channel_id=1, source_target_pairs={{0,4},{1,5},{2,6},{3,7},{4,8},{5,9},{6,10},{7,11},{8,12},{9,13},{1... | collective-permute-start | bytes 737288 | tf_op jit(solution)/shard_map/scatter/ppermute | solution.py:81
  187.6 6.9 %copy-start.5 = (s32[128,2]{0,1:T(2,128)S(1)}, s32[128,2]{0,1:T(2,128)}, u32[]{:S(2)}) copy-start(s32[128,2]{0,1:T(2,128)} %param.7) | copy-start | bytes 3076
  187.6 6.9 %copy-start.6 = (f32[128,2]{0,1:T(2,128)S(1)}, f32[128,2]{0,1:T(2,128)}, u32[]{:S(2)}) copy-start(f32[128,2]{0,1:T(2,128)} %param.8) | copy-start | bytes 3076
  187.6 31.9 %copy-start.1 = (bf16[128,3072]{1,0:T(8,128)(2,1)S(1)}, bf16[128,3072]{1,0:T(8,128)(2,1)}, u32[]{:S(2)}) copy-start(bf16[128,3072]{1,0:T(8,128)(2,1)} %param.6) | copy-start | bytes 2359300
  189.2 28.0 %all-to-all-start.2 = ((bf16[8,40,3072]{2,1,0:T(8,128)(2,1)}), bf16[8,40,3072]{2,1,0:T(8,128)(2,1)S(1)}, u32[]{:S(2)}, u32[]{:S(2)}) async-start(bf16[8,40,3072]{2,1,0:T(8,128)(2,1)} %broadcast_in_dim.20), calls=%async_computation.2 | async-start | bytes 3932160 | tf_op jit(solution)/shard_map/mix/all_to_all | solution.py:87
